TPU v7x, 32 devices: a whole 2x2x4 slice. The times are simulated.
32 devices in a mesh: gx: 8 (over z, x), gy: 4 (over y, core).
Axes of the slice: x: 2, y: 2, z: 4, core: 2. Of those that a mesh axis runs over, the one named last changes fastest.
Arguments:
- innovations: bfloat16 [32, 64, 128], P(('gx', 'gy')), may hold values from -18 to 18
- station_columns: int32 [32, 128], P(('gx', 'gy')), may hold values from 0 to 8191
- profile_counts: int32 [32, 32], P(('gx', 'gy')), may hold values from 0 to 4, as said below
- land_mask: int32 [64, 4096], P('gy', 'gx'), may hold values 0 or 1
- vertical_coef: float32 [32, 64, 4096], P(None, 'gy', 'gx'), may hold values from 0.3 to 30
- inverse_x: bfloat16 [2, 4096, 4096], P(None, None, 'gx')
- inverse_y: bfloat16 [2, 64, 64], replicated
Outputs:
- increment: bfloat16 [64, 64, 4096], P(None, 'gy', 'gx')
- equivalents: bfloat16 [32, 64, 128], P(('gx', 'gy'))
Inputs may be any that keep to these rules, and one draw needn't show every extreme that they name: `profile_counts`: every draw has one owner device that receives 4 live profiles from every device.
All inputs are finite; a program needn't handle non-finite values. No bound on the sum of `land_mask` on one device may be relied on, other than what follows from the above.
Results may differ from a plain program's by a relative error of at most 0.0061.
Values may be sent and summed in bfloat16 or wider, within the bound.
A program may use at most 64 MiB of HBM per device.

v0:
```python
import jax
import jax.numpy as jnp
from jax import lax
from jax.sharding import PartitionSpec as P

LEV = 32


def vertical_solve(rhs_field, coupling):
    levels = coupling.shape[0]
    zero_row = jnp.zeros_like(coupling[0])
    ratios = []
    partial_sol = []
    for level in range(levels):
        upper_coef = coupling[level + 1] if level + 1 < levels else zero_row
        diagonal = 1.0 + coupling[level] + upper_coef
        if level == 0:
            denominator = diagonal
            carried = rhs_field[:, 0]
        else:
            denominator = diagonal + coupling[level] * ratios[-1]
            carried = rhs_field[:, level] + coupling[level] * partial_sol[-1]
        ratios.append(-upper_coef / denominator)
        partial_sol.append(carried / denominator)
    solution = [partial_sol[-1]]
    for level in range(levels - 2, -1, -1):
        solution.append(partial_sol[level] - ratios[level] * solution[-1])
    return jnp.stack(solution[::-1], axis=1)


def body(
    innovations, station_columns, profile_counts, land_mask, vertical_coef, inverse_x, inverse_y
):
    layers = innovations.shape[1]
    devices_all = lax.axis_size(("gx", "gy"))
    devices_y = lax.axis_size("gy")
    capacity = innovations.shape[2] // devices_all
    slots = devices_all * capacity
    cells_y, cells_x = land_mask.shape
    cell_count = cells_y * cells_x
    tracers = inverse_x.shape[0]
    slot_index = lax.broadcasted_iota(jnp.int32, (devices_all, capacity), 1)
    live_flat = (slot_index < profile_counts[0][:, None]).reshape(slots)
    outgoing = jnp.where(live_flat[None, None, :], innovations, jnp.zeros((), jnp.bfloat16))
    arrived = lax.all_to_all(
        outgoing.reshape(layers, 1, devices_all, capacity),
        ("gx", "gy"),
        split_axis=2,
        concat_axis=1,
        tiled=True,
    )
    arrived = arrived.reshape(layers, slots)
    columns = station_columns[0]
    mask_flat = land_mask.reshape(cell_count)
    sea_slot = mask_flat[columns] > 0
    line_values = jnp.where(sea_slot[None, :], arrived, jnp.zeros((), jnp.bfloat16))
    line_columns = columns.reshape(1, slots)
    empty = jnp.zeros((tracers, layers // tracers, cells_y, cells_x), jnp.float32)
    values_piece = lax.all_gather(line_values, "gx", axis=1, tiled=True)
    columns_piece = lax.all_gather(line_columns, "gx", axis=1, tiled=True)
    sources = values_piece.shape[1] // slots

    def one_source(k, accum):
        block_values = lax.dynamic_slice_in_dim(values_piece, k * slots, slots, 1)
        block_columns = lax.dynamic_slice_in_dim(columns_piece, k * slots, slots, 1)[0]
        dense = (
            jnp.zeros((layers, cell_count), jnp.float32)
            .at[:, block_columns]
            .add(block_values.astype(jnp.float32))
        )
        dense = dense.astype(jnp.bfloat16).reshape(tracers, layers // tracers, cells_y, cells_x)
        source = k * slots // slots
        kernel_rows = lax.dynamic_slice_in_dim(inverse_x, source * cells_x, cells_x, 1)
        return accum + jnp.einsum(
            "tkjn,tnm->tkjm", dense, kernel_rows, preferred_element_type=jnp.float32
        )

    summed_x = lax.fori_loop(0, sources, one_source, empty)
    along_x = summed_x.astype(jnp.bfloat16).reshape(layers, cells_y, cells_x)
    rows_y = layers // devices_y
    tracer_y = lax.axis_index("gy") * rows_y // LEV
    matrix_y = lax.dynamic_index_in_dim(inverse_y, tracer_y, 0, keepdims=False)
    product = jnp.einsum(
        "rjc,jm->rmc",
        lax.all_to_all(along_x, "gy", split_axis=0, concat_axis=1, tiled=True),
        matrix_y,
        preferred_element_type=jnp.float32,
    ).astype(jnp.bfloat16)
    along_y = lax.all_to_all(product, "gy", split_axis=1, concat_axis=0, tiled=True)
    mask_field = mask_flat.astype(jnp.float32)
    column_field = along_y.astype(jnp.float32).reshape(2, LEV, cell_count)
    solved = vertical_solve(column_field, vertical_coef.reshape(LEV, cell_count))
    increment = (
        (solved * mask_field[None, None, :]).astype(jnp.bfloat16).reshape(layers, cells_y, cells_x)
    )
    picked = increment.reshape(layers, cell_count)[:, columns]
    returned = lax.all_to_all(
        picked.reshape(layers, 1, devices_all, capacity),
        ("gx", "gy"),
        split_axis=2,
        concat_axis=1,
        tiled=True,
    )
    returned = returned.reshape(1, layers, slots)
    equivalents = jnp.where(live_flat[None, None, :], returned, jnp.zeros((), jnp.bfloat16))
    return (increment, equivalents)


def solution(mesh):
    in_specs = (
        P(("gx", "gy"), None, None),
        P(("gx", "gy"), None),
        P(("gx", "gy"), None),
        P("gy", "gx"),
        P(None, "gy", "gx"),
        P(None, None, "gx"),
        P(),
    )
    out_specs = (P(None, "gy", "gx"), P(("gx", "gy"), None, None))
    return jax.shard_map(body, mesh=mesh, in_specs=in_specs, out_specs=out_specs, check_vma=False)
```

profile of v0, /device:TPU:0, one launch (start us, length us, event | category | flops | bytes accessed | tf_op | source)
XLA Modules:
  0.0 227.5 jit_solution(4282245985463795626)
XLA Ops:
  3.2 7.3 %all-to-all-start = ((bf16[32,2,128]{2,1,0:T(2,128)(2,1)}), bf16[32,2,128]{2,1,0:T(2,128)(2,1)S(1)}, u32[]{:S(2)}, u32[]{:S(2)}) async-start(bf16[32,2,128]{2,1,0:T(2,128)(2,1)} %reshape.25774), calls=%async_computation | async-start | bytes 32768 | tf_op jit(solution)/shard_map/all_to_all | solution.py:45
  10.5 1.6 slice_bitcast_fusion
  12.1 1.7 slice_bitcast_fusion.1
  25.5 1.4 negate_divide_fusion.13
  26.9 1.4 negate_divide_fusion.10
  32.4 20.7 %all_gather.6 = s32[1,1024]{1,0:T(1,128)S(1)} all-gather(s32[1,128]{1,0:T(1,128)S(1)} %copy-done.105), channel_id=1, replica_groups=mesh['gx'=8,'gy'=4] {'gx'}, dimensions={1}, use_global_device_ids=true | all-gather | bytes 4608 | tf_op jit(solution)/shard_map/all_gather | solution.py:60
  53.2 30.9 %all_gather.7 = bf16[64,1024]{0,1:T(8,128)(2,1)S(1)} all-gather(bf16[64,128]{0,1:T(8,128)(2,1)S(1)} %broadcast_select_fusion.2), channel_id=1, replica_groups=mesh['gx'=8,'gy'=4] {'gx'}, dimensions={1}, use_global_device_ids=true | all-gather | bytes 147456 | tf_op jit(solution)/shard_map/all_gather | solution.py:59
  84.2 70.0 %while.16 = (s32[]{:T(128)}, f32[2,32,16,512]{3,2,1,0:T(8,128)S(1)}, s32[1,1024]{1,0:T(1,128)S(1)}, bf16[64,1024]{0,1:T(8,128)(2,1)S(1)}, bf16[2,4096,512]{2,1,0...) while((s32[]{:T(128)}, ...), condition=%wide.region_2.3_spmd.clone, body=%wide.region_0.2_spmd.clone.sunk | while | flops 537936256 | bytes 13665692 | solution.py:78
  84.2 3.3 %scatter_custom_fusion.6 = f32[64,8192]{0,1:T(8,128)} fusion(s32[128]{0:T(128)S(1)} %fusion.86, f32[]{:T(128)} %constant.125.clone.3..sunk, bf16[64,1024]{0,1:T(8,128)(2,1)S(1)} %get-tuple-element.392, s32[]{:T(128)} %constant.139.clone.1..sunk, s32[]{:T(128)S(6)} %select_n.115), kind=kCustom, calls=%fused_computation.4.clone.1 | custom fusion | flops 16384 | bytes 2129932 | tf_op jit(solution)/shard_map/while/body/eval_jaxpr/scatter-add | solution.py:69
  87.4 2.6 %copy.337 = bf16[64,8192]{1,0:T(8,128)(2,1)S(1)} copy(f32[64,8192]{0,1:T(8,128)} %scatter_custom_fusion.6) | data formatting | bytes 3145728 | tf_op jit(solution)/shard_map/while/body/eval_jaxpr/scatter-add | solution.py:69
  90.4 2.5 %select_add_fusion.2 = f32[2,32,16,512]{3,2,1,0:T(8,128)S(1)} fusion(f32[2,32,16,512]{3,2,1,0:T(8,128)S(1)} %get-tuple-element.375, bf16[2,4096,512]{2,1,0:T(8,128)(2,1)} %get-tuple-element.393, s32[]{:T(128)S(6)} %select_n.114, pred[]{:T(512)S(6)} %compare.13, bf16[2,32,16,512]{3,2,1,0:T(8,128)(2,1)S(1)} %bitcast.183), kind=kOutput, calls=%fused_computation.3.clone.1 | convolution fusion | flops 537919488 | bytes 6291461 | tf_op jit(solution)/shard_map/while/body/eval_jaxpr/tkjn,tnm->tkjm/dot_general | solution.py:74
  92.9 3.3 %scatter_custom_fusion.6 = f32[64,8192]{0,1:T(8,128)} fusion(s32[128]{0:T(128)S(1)} %fusion.86, f32[]{:T(128)} %constant.125.clone.3..sunk, bf16[64,1024]{0,1:T(8,128)(2,1)S(1)} %get-tuple-element.392, s32[]{:T(128)} %constant.139.clone.1..sunk, s32[]{:T(128)S(6)} %select_n.115), kind=kCustom, calls=%fused_computation.4.clone.1 | custom fusion | flops 16384 | bytes 2129932 | tf_op jit(solution)/shard_map/while/body/eval_jaxpr/scatter-add | solution.py:69
  96.2 2.6 %copy.337 = bf16[64,8192]{1,0:T(8,128)(2,1)S(1)} copy(f32[64,8192]{0,1:T(8,128)} %scatter_custom_fusion.6) | data formatting | bytes 3145728 | tf_op jit(solution)/shard_map/while/body/eval_jaxpr/scatter-add | solution.py:69
  99.1 2.5 %select_add_fusion.2 = f32[2,32,16,512]{3,2,1,0:T(8,128)S(1)} fusion(f32[2,32,16,512]{3,2,1,0:T(8,128)S(1)} %get-tuple-element.375, bf16[2,4096,512]{2,1,0:T(8,128)(2,1)} %get-tuple-element.393, s32[]{:T(128)S(6)} %select_n.114, pred[]{:T(512)S(6)} %compare.13, bf16[2,32,16,512]{3,2,1,0:T(8,128)(2,1)S(1)} %bitcast.183), kind=kOutput, calls=%fused_computation.3.clone.1 | convolution fusion | flops 537919488 | bytes 6291461 | tf_op jit(solution)/shard_map/while/body/eval_jaxpr/tkjn,tnm->tkjm/dot_general | solution.py:74
  101.7 3.3 %scatter_custom_fusion.6 = f32[64,8192]{0,1:T(8,128)} fusion(s32[128]{0:T(128)S(1)} %fusion.86, f32[]{:T(128)} %constant.125.clone.3..sunk, bf16[64,1024]{0,1:T(8,128)(2,1)S(1)} %get-tuple-element.392, s32[]{:T(128)} %constant.139.clone.1..sunk, s32[]{:T(128)S(6)} %select_n.115), kind=kCustom, calls=%fused_computation.4.clone.1 | custom fusion | flops 16384 | bytes 2129932 | tf_op jit(solution)/shard_map/while/body/eval_jaxpr/scatter-add | solution.py:69
  105.0 2.6 %copy.337 = bf16[64,8192]{1,0:T(8,128)(2,1)S(1)} copy(f32[64,8192]{0,1:T(8,128)} %scatter_custom_fusion.6) | data formatting | bytes 3145728 | tf_op jit(solution)/shard_map/while/body/eval_jaxpr/scatter-add | solution.py:69
  107.9 2.5 %select_add_fusion.2 = f32[2,32,16,512]{3,2,1,0:T(8,128)S(1)} fusion(f32[2,32,16,512]{3,2,1,0:T(8,128)S(1)} %get-tuple-element.375, bf16[2,4096,512]{2,1,0:T(8,128)(2,1)} %get-tuple-element.393, s32[]{:T(128)S(6)} %select_n.114, pred[]{:T(512)S(6)} %compare.13, bf16[2,32,16,512]{3,2,1,0:T(8,128)(2,1)S(1)} %bitcast.183), kind=kOutput, calls=%fused_computation.3.clone.1 | convolution fusion | flops 537919488 | bytes 6291461 | tf_op jit(solution)/shard_map/while/body/eval_jaxpr/tkjn,tnm->tkjm/dot_general | solution.py:74
  110.4 3.3 %scatter_custom_fusion.6 = f32[64,8192]{0,1:T(8,128)} fusion(s32[128]{0:T(128)S(1)} %fusion.86, f32[]{:T(128)} %constant.125.clone.3..sunk, bf16[64,1024]{0,1:T(8,128)(2,1)S(1)} %get-tuple-element.392, s32[]{:T(128)} %constant.139.clone.1..sunk, s32[]{:T(128)S(6)} %select_n.115), kind=kCustom, calls=%fused_computation.4.clone.1 | custom fusion | flops 16384 | bytes 2129932 | tf_op jit(solution)/shard_map/while/body/eval_jaxpr/scatter-add | solution.py:69
  113.7 2.6 %copy.337 = bf16[64,8192]{1,0:T(8,128)(2,1)S(1)} copy(f32[64,8192]{0,1:T(8,128)} %scatter_custom_fusion.6) | data formatting | bytes 3145728 | tf_op jit(solution)/shard_map/while/body/eval_jaxpr/scatter-add | solution.py:69
  116.6 2.5 %select_add_fusion.2 = f32[2,32,16,512]{3,2,1,0:T(8,128)S(1)} fusion(f32[2,32,16,512]{3,2,1,0:T(8,128)S(1)} %get-tuple-element.375, bf16[2,4096,512]{2,1,0:T(8,128)(2,1)} %get-tuple-element.393, s32[]{:T(128)S(6)} %select_n.114, pred[]{:T(512)S(6)} %compare.13, bf16[2,32,16,512]{3,2,1,0:T(8,128)(2,1)S(1)} %bitcast.183), kind=kOutput, calls=%fused_computation.3.clone.1 | convolution fusion | flops 537919488 | bytes 6291461 | tf_op jit(solution)/shard_map/while/body/eval_jaxpr/tkjn,tnm->tkjm/dot_general | solution.py:74
  119.2 3.3 %scatter_custom_fusion.6 = f32[64,8192]{0,1:T(8,128)} fusion(s32[128]{0:T(128)S(1)} %fusion.86, f32[]{:T(128)} %constant.125.clone.3..sunk, bf16[64,1024]{0,1:T(8,128)(2,1)S(1)} %get-tuple-element.392, s32[]{:T(128)} %constant.139.clone.1..sunk, s32[]{:T(128)S(6)} %select_n.115), kind=kCustom, calls=%fused_computation.4.clone.1 | custom fusion | flops 16384 | bytes 2129932 | tf_op jit(solution)/shard_map/while/body/eval_jaxpr/scatter-add | solution.py:69
  122.5 2.6 %copy.337 = bf16[64,8192]{1,0:T(8,128)(2,1)S(1)} copy(f32[64,8192]{0,1:T(8,128)} %scatter_custom_fusion.6) | data formatting | bytes 3145728 | tf_op jit(solution)/shard_map/while/body/eval_jaxpr/scatter-add | solution.py:69
  125.4 2.5 %select_add_fusion.2 = f32[2,32,16,512]{3,2,1,0:T(8,128)S(1)} fusion(f32[2,32,16,512]{3,2,1,0:T(8,128)S(1)} %get-tuple-element.375, bf16[2,4096,512]{2,1,0:T(8,128)(2,1)} %get-tuple-element.393, s32[]{:T(128)S(6)} %select_n.114, pred[]{:T(512)S(6)} %compare.13, bf16[2,32,16,512]{3,2,1,0:T(8,128)(2,1)S(1)} %bitcast.183), kind=kOutput, calls=%fused_computation.3.clone.1 | convolution fusion | flops 537919488 | bytes 6291461 | tf_op jit(solution)/shard_map/while/body/eval_jaxpr/tkjn,tnm->tkjm/dot_general | solution.py:74
  128.0 3.3 %scatter_custom_fusion.6 = f32[64,8192]{0,1:T(8,128)} fusion(s32[128]{0:T(128)S(1)} %fusion.86, f32[]{:T(128)} %constant.125.clone.3..sunk, bf16[64,1024]{0,1:T(8,128)(2,1)S(1)} %get-tuple-element.392, s32[]{:T(128)} %constant.139.clone.1..sunk, s32[]{:T(128)S(6)} %select_n.115), kind=kCustom, calls=%fused_computation.4.clone.1 | custom fusion | flops 16384 | bytes 2129932 | tf_op jit(solution)/shard_map/while/body/eval_jaxpr/scatter-add | solution.py:69
  131.2 2.6 %copy.337 = bf16[64,8192]{1,0:T(8,128)(2,1)S(1)} copy(f32[64,8192]{0,1:T(8,128)} %scatter_custom_fusion.6) | data formatting | bytes 3145728 | tf_op jit(solution)/shard_map/while/body/eval_jaxpr/scatter-add | solution.py:69
  134.2 2.5 %select_add_fusion.2 = f32[2,32,16,512]{3,2,1,0:T(8,128)S(1)} fusion(f32[2,32,16,512]{3,2,1,0:T(8,128)S(1)} %get-tuple-element.375, bf16[2,4096,512]{2,1,0:T(8,128)(2,1)} %get-tuple-element.393, s32[]{:T(128)S(6)} %select_n.114, pred[]{:T(512)S(6)} %compare.13, bf16[2,32,16,512]{3,2,1,0:T(8,128)(2,1)S(1)} %bitcast.183), kind=kOutput, calls=%fused_computation.3.clone.1 | convolution fusion | flops 537919488 | bytes 6291461 | tf_op jit(solution)/shard_map/while/body/eval_jaxpr/tkjn,tnm->tkjm/dot_general | solution.py:74
  136.7 3.3 %scatter_custom_fusion.6 = f32[64,8192]{0,1:T(8,128)} fusion(s32[128]{0:T(128)S(1)} %fusion.86, f32[]{:T(128)} %constant.125.clone.3..sunk, bf16[64,1024]{0,1:T(8,128)(2,1)S(1)} %get-tuple-element.392, s32[]{:T(128)} %constant.139.clone.1..sunk, s32[]{:T(128)S(6)} %select_n.115), kind=kCustom, calls=%fused_computation.4.clone.1 | custom fusion | flops 16384 | bytes 2129932 | tf_op jit(solution)/shard_map/while/body/eval_jaxpr/scatter-add | solution.py:69
  140.0 2.6 %copy.337 = bf16[64,8192]{1,0:T(8,128)(2,1)S(1)} copy(f32[64,8192]{0,1:T(8,128)} %scatter_custom_fusion.6) | data formatting | bytes 3145728 | tf_op jit(solution)/shard_map/while/body/eval_jaxpr/scatter-add | solution.py:69
  142.9 2.5 %select_add_fusion.2 = f32[2,32,16,512]{3,2,1,0:T(8,128)S(1)} fusion(f32[2,32,16,512]{3,2,1,0:T(8,128)S(1)} %get-tuple-element.375, bf16[2,4096,512]{2,1,0:T(8,128)(2,1)} %get-tuple-element.393, s32[]{:T(128)S(6)} %select_n.114, pred[]{:T(512)S(6)} %compare.13, bf16[2,32,16,512]{3,2,1,0:T(8,128)(2,1)S(1)} %bitcast.183), kind=kOutput, calls=%fused_computation.3.clone.1 | convolution fusion | flops 537919488 | bytes 6291461 | tf_op jit(solution)/shard_map/while/body/eval_jaxpr/tkjn,tnm->tkjm/dot_general | solution.py:74
  145.5 3.3 %scatter_custom_fusion.6 = f32[64,8192]{0,1:T(8,128)} fusion(s32[128]{0:T(128)S(1)} %fusion.86, f32[]{:T(128)} %constant.125.clone.3..sunk, bf16[64,1024]{0,1:T(8,128)(2,1)S(1)} %get-tuple-element.392, s32[]{:T(128)} %constant.139.clone.1..sunk, s32[]{:T(128)S(6)} %select_n.115), kind=kCustom, calls=%fused_computation.4.clone.1 | custom fusion | flops 16384 | bytes 2129932 | tf_op jit(solution)/shard_map/while/body/eval_jaxpr/scatter-add | solution.py:69
  148.7 2.6 %copy.337 = bf16[64,8192]{1,0:T(8,128)(2,1)S(1)} copy(f32[64,8192]{0,1:T(8,128)} %scatter_custom_fusion.6) | data formatting | bytes 3145728 | tf_op jit(solution)/shard_map/while/body/eval_jaxpr/scatter-add | solution.py:69
  151.7 2.5 %select_add_fusion.2 = f32[2,32,16,512]{3,2,1,0:T(8,128)S(1)} fusion(f32[2,32,16,512]{3,2,1,0:T(8,128)S(1)} %get-tuple-element.375, bf16[2,4096,512]{2,1,0:T(8,128)(2,1)} %get-tuple-element.393, s32[]{:T(128)S(6)} %select_n.114, pred[]{:T(512)S(6)} %compare.13, bf16[2,32,16,512]{3,2,1,0:T(8,128)(2,1)S(1)} %bitcast.183), kind=kOutput, calls=%fused_computation.3.clone.1 | convolution fusion | flops 537919488 | bytes 6291461 | tf_op jit(solution)/shard_map/while/body/eval_jaxpr/tkjn,tnm->tkjm/dot_general | solution.py:74
  155.4 3.5 %all-to-all-start.1 = ((bf16[64,16,512]{2,1,0:T(8,128)(2,1)}), bf16[64,16,512]{2,1,0:T(8,128)(2,1)S(1)}, u32[]{:S(2)}, u32[]{:S(2)}) async-start(bf16[64,16,512]{2,1,0:T(8,128)(2,1)} %bitcast.8), calls=%async_computation.1 | async-start | bytes 2097152 | tf_op jit(solution)/shard_map/all_to_all | solution.py:85
  161.6 11.7 %all-to-all-done.1 = bf16[64,16,512]{2,1,0:T(8,128)(2,1)S(1)} async-done(((bf16[64,16,512]{2,1,0:T(8,128)(2,1)}), bf16[64,16,512]{2,1,0:T(8,128)(2,1)S(1)}, u32[]{:S(2)}, u32[]{:S(2)}) %all-to-all-start.1) | async-done | bytes 1048608 | tf_op jit(solution)/shard_map/all_to_all | solution.py:85
  174.0 1.5 copy.79
  175.5 3.7 %all-to-all-start.2 = ((bf16[16,64,512]{2,0,1:T(8,128)(2,1)}), bf16[16,64,512]{2,0,1:T(8,128)(2,1)S(1)}, u32[]{:S(2)}, u32[]{:S(2)}) async-start(bf16[16,64,512]{2,0,1:T(8,128)(2,1)} %copy.79), calls=%async_computation.2 | async-start | bytes 2097152 | tf_op jit(solution)/shard_map/all_to_all | solution.py:89
  182.4 11.0 %all-to-all-done.2 = bf16[16,64,512]{2,0,1:T(8,128)(2,1)S(1)} async-done(((bf16[16,64,512]{2,0,1:T(8,128)(2,1)}), bf16[16,64,512]{2,0,1:T(8,128)(2,1)S(1)}, u32[]{:S(2)}, u32[]{:S(2)}) %all-to-all-start.2) | async-done | bytes 1048608 | tf_op jit(solution)/shard_map/all_to_all | solution.py:89
  193.5 1.9 copy.334
  195.4 1.7 reshape.25740
  198.2 1.2 fusion.76
  199.8 4.9 %fusion.18 = (f32[2,1,8192]{2,0,1:T(2,128)S(1)}, f32[2,1,8192]{2,0,1:T(2,128)S(1)}, f32[2,1,8192]{2,0,1:T(2,128)S(1)}, f32[2,1,8192]{2,0,1:T(2,128)S(1)}, f32[2,...) fusion(f32[2,1,8192]{2,1,0:T(1,128)S(1)} %get-tuple-element.266, ...), kind=kLoop, calls=%fused_computation.65 | loop fusion | flops 1343488 | bytes 5406720 | tf_op jit(solution)/shard_map/div | solution.py:24
  204.9 2.8 %constant_dynamic-update-slice_fusion.31 = (f32[2,32,8192]{2,0,1:T(2,128)S(1)}, f32[2,1,8192]{2,0,1:T(2,128)S(1)}, f32[2,1,8192]{2,0,1:T(2,128)S(1)}, f32[2,1,81...) fusion(f32[8192]{0:T(1024)} %get-tuple-element.189, ...), kind=kLoop, calls=%fused_computation.55 | loop fusion | flops 1228799 | bytes 4521984
  209.4 1.2 copy.113
  212.0 1.8 copy.115
  213.8 2.5 %gather_fusion.1 = bf16[128,64]{1,0:T(8,128)(2,1)S(1)} fusion(bf16[64,8192]{0,1:T(8,128)(2,1)} %copy.115, s32[1024]{0:T(1024)S(1)} %pad_clamp_fusion), kind=kCustom, calls=%fused_computation.1 | custom fusion | bytes 33280 | tf_op jit(solution)/shard_map/gather | solution.py:96
  217.0 2.5 %all-to-all-start.3 = ((bf16[32,2,128]{2,1,0:T(2,128)(2,1)}), bf16[32,2,128]{2,1,0:T(2,128)(2,1)S(1)}, u32[]{:S(2)}, u32[]{:S(2)}) async-start(bf16[32,2,128]{2,1,0:T(2,128)(2,1)} %reshape.25776), calls=%async_computation.3 | async-start | bytes 32768 | tf_op jit(solution)/shard_map/all_to_all | solution.py:97
  219.5 1.3 fusion.11
  220.8 5.8 %all-to-all-done.3 = bf16[32,2,128]{2,1,0:T(2,128)(2,1)S(1)} async-done(((bf16[32,2,128]{2,1,0:T(2,128)(2,1)}), bf16[32,2,128]{2,1,0:T(2,128)(2,1)S(1)}, u32[]{:S(2)}, u32[]{:S(2)}) %all-to-all-start.3) | async-done | bytes 16416 | tf_op jit(solution)/shard_map/all_to_all | solution.py:97
  (346 shorter events, 33.5 us)
Async XLA Ops:
  0.6 172.8 %copy-start = (bf16[2,64,64]{2,1,0:T(8,128)(2,1)S(1)}, bf16[2,64,64]{2,1,0:T(8,128)(2,1)}, u32[]{:S(2)}) copy-start(bf16[2,64,64]{2,1,0:T(8,128)(2,1)} %param.15) | copy-start | bytes 49156
  0.6 13.2 %copy-start.102 = (s32[16,512]{1,0:T(8,128)S(1)}, s32[16,512]{1,0:T(8,128)}, u32[]{:S(2)}) copy-start(s32[16,512]{1,0:T(8,128)} %param.12) | copy-start | bytes 98308
  0.7 13.2 %copy-start.105 = (s32[1,128]{1,0:T(1,128)S(1)}, s32[1,128]{1,0:T(1,128)}, u32[]{:S(2)}) copy-start(s32[1,128]{1,0:T(1,128)} %param.10) | copy-start | bytes 1540
  3.2 49.9 %all-to-all-start = ((bf16[32,2,128]{2,1,0:T(2,128)(2,1)}), bf16[32,2,128]{2,1,0:T(2,128)(2,1)S(1)}, u32[]{:S(2)}, u32[]{:S(2)}) async-start(bf16[32,2,128]{2,1,0:T(2,128)(2,1)} %reshape.25774), calls=%async_computation | async-start | bytes 32768 | tf_op jit(solution)/shard_map/all_to_all | solution.py:45
  13.8 9.7 %copy-start.47 = (f32[2,4,8,128]{3,1,2,0:T(4,128)}, f32[2,4,8,128]{3,1,2,0:T(4,128)S(1)}, u32[]{:S(2)}) copy-start(f32[2,4,8,128]{3,1,2,0:T(4,128)S(1)} %copy.154) | copy-start | bytes 98308
  13.9 17.5 %copy-start.1 = (f32[2,4,8,128]{3,1,2,0:T(4,128)}, f32[2,4,8,128]{3,1,2,0:T(4,128)S(1)}, u32[]{:S(2)}) copy-start(f32[2,4,8,128]{3,1,2,0:T(4,128)S(1)} %copy.177) | copy-start | bytes 98308
  14.0 17.5 %copy-start.3 = (f32[2,4,8,128]{3,1,2,0:T(4,128)}, f32[2,4,8,128]{3,1,2,0:T(4,128)S(1)}, u32[]{:S(2)}) copy-start(f32[2,4,8,128]{3,1,2,0:T(4,128)S(1)} %copy.176) | copy-start | bytes 98308
  14.0 15.6 %copy-start.5 = (f32[2,4,8,128]{3,1,2,0:T(4,128)}, f32[2,4,8,128]{3,1,2,0:T(4,128)S(1)}, u32[]{:S(2)}) copy-start(f32[2,4,8,128]{3,1,2,0:T(4,128)S(1)} %copy.175) | copy-start | bytes 98308
  14.0 14.9 %copy-start.7 = (f32[2,4,8,128]{3,1,2,0:T(4,128)}, f32[2,4,8,128]{3,1,2,0:T(4,128)S(1)}, u32[]{:S(2)}) copy-start(f32[2,4,8,128]{3,1,2,0:T(4,128)S(1)} %copy.174) | copy-start | bytes 98308
  14.1 14.3 %copy-start.9 = (f32[2,4,8,128]{3,1,2,0:T(4,128)}, f32[2,4,8,128]{3,1,2,0:T(4,128)S(1)}, u32[]{:S(2)}) copy-start(f32[2,4,8,128]{3,1,2,0:T(4,128)S(1)} %copy.173) | copy-start | bytes 98308
  14.1 12.8 %copy-start.11 = (f32[2,4,8,128]{3,1,2,0:T(4,128)}, f32[2,4,8,128]{3,1,2,0:T(4,128)S(1)}, u32[]{:S(2)}) copy-start(f32[2,4,8,128]{3,1,2,0:T(4,128)S(1)} %copy.172) | copy-start | bytes 98308
  14.1 12.8 %copy-start.13 = (f32[2,4,8,128]{3,1,2,0:T(4,128)}, f32[2,4,8,128]{3,1,2,0:T(4,128)S(1)}, u32[]{:S(2)}) copy-start(f32[2,4,8,128]{3,1,2,0:T(4,128)S(1)} %copy.171) | copy-start | bytes 98308
  14.1 14.2 %copy-start.15 = (f32[2,4,8,128]{3,1,2,0:T(4,128)}, f32[2,4,8,128]{3,1,2,0:T(4,128)S(1)}, u32[]{:S(2)}) copy-start(f32[2,4,8,128]{3,1,2,0:T(4,128)S(1)} %copy.170) | copy-start | bytes 98308
  14.2 14.1 %copy-start.17 = (f32[2,4,8,128]{3,1,2,0:T(4,128)}, f32[2,4,8,128]{3,1,2,0:T(4,128)S(1)}, u32[]{:S(2)}) copy-start(f32[2,4,8,128]{3,1,2,0:T(4,128)S(1)} %copy.169) | copy-start | bytes 98308
  14.2 14.1 %copy-start.19 = (f32[2,4,8,128]{3,1,2,0:T(4,128)}, f32[2,4,8,128]{3,1,2,0:T(4,128)S(1)}, u32[]{:S(2)}) copy-start(f32[2,4,8,128]{3,1,2,0:T(4,128)S(1)} %copy.168) | copy-start | bytes 98308
  14.2 14.1 %copy-start.21 = (f32[2,4,8,128]{3,1,2,0:T(4,128)}, f32[2,4,8,128]{3,1,2,0:T(4,128)S(1)}, u32[]{:S(2)}) copy-start(f32[2,4,8,128]{3,1,2,0:T(4,128)S(1)} %copy.167) | copy-start | bytes 98308
  14.3 14.7 %copy-start.23 = (f32[2,4,8,128]{3,1,2,0:T(4,128)}, f32[2,4,8,128]{3,1,2,0:T(4,128)S(1)}, u32[]{:S(2)}) copy-start(f32[2,4,8,128]{3,1,2,0:T(4,128)S(1)} %copy.166) | copy-start | bytes 98308
  14.3 15.3 %copy-start.25 = (f32[2,4,8,128]{3,1,2,0:T(4,128)}, f32[2,4,8,128]{3,1,2,0:T(4,128)S(1)}, u32[]{:S(2)}) copy-start(f32[2,4,8,128]{3,1,2,0:T(4,128)S(1)} %copy.165) | copy-start | bytes 98308
  14.3 15.3 %copy-start.27 = (f32[2,4,8,128]{3,1,2,0:T(4,128)}, f32[2,4,8,128]{3,1,2,0:T(4,128)S(1)}, u32[]{:S(2)}) copy-start(f32[2,4,8,128]{3,1,2,0:T(4,128)S(1)} %copy.164) | copy-start | bytes 98308
  14.3 15.3 %copy-start.29 = (f32[2,4,8,128]{3,1,2,0:T(4,128)}, f32[2,4,8,128]{3,1,2,0:T(4,128)S(1)}, u32[]{:S(2)}) copy-start(f32[2,4,8,128]{3,1,2,0:T(4,128)S(1)} %copy.163) | copy-start | bytes 98308
  14.4 15.3 %copy-start.31 = (f32[2,4,8,128]{3,1,2,0:T(4,128)}, f32[2,4,8,128]{3,1,2,0:T(4,128)S(1)}, u32[]{:S(2)}) copy-start(f32[2,4,8,128]{3,1,2,0:T(4,128)S(1)} %copy.162) | copy-start | bytes 98308
  14.4 15.9 %copy-start.33 = (f32[2,4,8,128]{3,1,2,0:T(4,128)}, f32[2,4,8,128]{3,1,2,0:T(4,128)S(1)}, u32[]{:S(2)}) copy-start(f32[2,4,8,128]{3,1,2,0:T(4,128)S(1)} %copy.161) | copy-start | bytes 98308
  14.4 17.0 %copy-start.35 = (f32[2,4,8,128]{3,1,2,0:T(4,128)}, f32[2,4,8,128]{3,1,2,0:T(4,128)S(1)}, u32[]{:S(2)}) copy-start(f32[2,4,8,128]{3,1,2,0:T(4,128)S(1)} %copy.160) | copy-start | bytes 98308
  14.4 17.0 %copy-start.37 = (f32[2,4,8,128]{3,1,2,0:T(4,128)}, f32[2,4,8,128]{3,1,2,0:T(4,128)S(1)}, u32[]{:S(2)}) copy-start(f32[2,4,8,128]{3,1,2,0:T(4,128)S(1)} %copy.159) | copy-start | bytes 98308
  14.5 17.0 %copy-start.39 = (f32[2,4,8,128]{3,1,2,0:T(4,128)}, f32[2,4,8,128]{3,1,2,0:T(4,128)S(1)}, u32[]{:S(2)}) copy-start(f32[2,4,8,128]{3,1,2,0:T(4,128)S(1)} %copy.158) | copy-start | bytes 98308
  14.5 17.0 %copy-start.41 = (f32[2,4,8,128]{3,1,2,0:T(4,128)}, f32[2,4,8,128]{3,1,2,0:T(4,128)S(1)}, u32[]{:S(2)}) copy-start(f32[2,4,8,128]{3,1,2,0:T(4,128)S(1)} %copy.157) | copy-start | bytes 98308
  14.5 16.9 %copy-start.43 = (f32[2,4,8,128]{3,1,2,0:T(4,128)}, f32[2,4,8,128]{3,1,2,0:T(4,128)S(1)}, u32[]{:S(2)}) copy-start(f32[2,4,8,128]{3,1,2,0:T(4,128)S(1)} %copy.156) | copy-start | bytes 98308
  14.6 16.9 %copy-start.45 = (f32[2,4,8,128]{3,1,2,0:T(4,128)}, f32[2,4,8,128]{3,1,2,0:T(4,128)S(1)}, u32[]{:S(2)}) copy-start(f32[2,4,8,128]{3,1,2,0:T(4,128)S(1)} %copy.155) | copy-start | bytes 98308
  15.9 16.3 %copy-start.61 = (f32[8192]{0:T(1024)}, f32[8192]{0:T(1024)S(1)}, u32[]{:S(2)}) copy-start(f32[8192]{0:T(1024)S(1)} %get-tuple-element.192) | copy-start | bytes 98308
  15.9 16.3 %copy-start.63 = (f32[8192]{0:T(1024)}, f32[8192]{0:T(1024)S(1)}, u32[]{:S(2)}) copy-start(f32[8192]{0:T(1024)S(1)} %get-tuple-element.193) | copy-start | bytes 98308
  16.5 15.7 %copy-start.65 = (f32[8192]{0:T(1024)}, f32[8192]{0:T(1024)S(1)}, u32[]{:S(2)}) copy-start(f32[8192]{0:T(1024)S(1)} %get-tuple-element.195) | copy-start | bytes 98308
  16.5 15.7 %copy-start.67 = (f32[8192]{0:T(1024)}, f32[8192]{0:T(1024)S(1)}, u32[]{:S(2)}) copy-start(f32[8192]{0:T(1024)S(1)} %get-tuple-element.196) | copy-start | bytes 98308
  17.8 14.4 %copy-start.69 = (f32[8192]{0:T(1024)}, f32[8192]{0:T(1024)S(1)}, u32[]{:S(2)}) copy-start(f32[8192]{0:T(1024)S(1)} %get-tuple-element.198) | copy-start | bytes 98308
  17.8 14.4 %copy-start.71 = (f32[8192]{0:T(1024)}, f32[8192]{0:T(1024)S(1)}, u32[]{:S(2)}) copy-start(f32[8192]{0:T(1024)S(1)} %get-tuple-element.199) | copy-start | bytes 98308
  19.1 13.2 %copy-start.72 = (f32[8192]{0:T(1024)}, f32[8192]{0:T(1024)S(1)}, u32[]{:S(2)}) copy-start(f32[8192]{0:T(1024)S(1)} %get-tuple-element.201) | copy-start | bytes 98308
  19.1 13.2 %copy-start.73 = (f32[8192]{0:T(1024)}, f32[8192]{0:T(1024)S(1)}, u32[]{:S(2)}) copy-start(f32[8192]{0:T(1024)S(1)} %get-tuple-element.202) | copy-start | bytes 98308
  20.3 11.9 %copy-start.74 = (f32[8192]{0:T(1024)}, f32[8192]{0:T(1024)S(1)}, u32[]{:S(2)}) copy-start(f32[8192]{0:T(1024)S(1)} %get-tuple-element.204) | copy-start | bytes 98308
  20.3 11.9 %copy-start.75 = (f32[8192]{0:T(1024)}, f32[8192]{0:T(1024)S(1)}, u32[]{:S(2)}) copy-start(f32[8192]{0:T(1024)S(1)} %get-tuple-element.205) | copy-start | bytes 98308
  21.6 10.6 %copy-start.76 = (f32[8192]{0:T(1024)}, f32[8192]{0:T(1024)S(1)}, u32[]{:S(2)}) copy-start(f32[8192]{0:T(1024)S(1)} %get-tuple-element.207) | copy-start | bytes 98308
  21.6 10.6 %copy-start.77 = (f32[8192]{0:T(1024)}, f32[8192]{0:T(1024)S(1)}, u32[]{:S(2)}) copy-start(f32[8192]{0:T(1024)S(1)} %get-tuple-element.208) | copy-start | bytes 98308
  22.9 9.4 %copy-start.79 = (f32[8192]{0:T(1024)}, f32[8192]{0:T(1024)S(1)}, u32[]{:S(2)}) copy-start(f32[8192]{0:T(1024)S(1)} %get-tuple-element.211) | copy-start | bytes 98308
  155.4 18.0 %all-to-all-start.1 = ((bf16[64,16,512]{2,1,0:T(8,128)(2,1)}), bf16[64,16,512]{2,1,0:T(8,128)(2,1)S(1)}, u32[]{:S(2)}, u32[]{:S(2)}) async-start(bf16[64,16,512]{2,1,0:T(8,128)(2,1)} %bitcast.8), calls=%async_computation.1 | async-start | bytes 2097152 | tf_op jit(solution)/shard_map/all_to_all | solution.py:85
  160.3 13.6 %copy-start.92 = (f32[8192]{0:T(1024)}, f32[8192]{0:T(1024)S(1)}, u32[]{:S(2)}) copy-start(f32[8192]{0:T(1024)S(1)} %get-tuple-element.228) | copy-start | bytes 98308
  160.3 13.6 %copy-start.93 = (f32[8192]{0:T(1024)}, f32[8192]{0:T(1024)S(1)}, u32[]{:S(2)}) copy-start(f32[8192]{0:T(1024)S(1)} %get-tuple-element.229) | copy-start | bytes 98308
  161.6 17.6 %copy-start.94 = (f32[8192]{0:T(1024)}, f32[8192]{0:T(1024)S(1)}, u32[]{:S(2)}) copy-start(f32[8192]{0:T(1024)S(1)} %get-tuple-element.232) | copy-start | bytes 98308
  161.6 19.5 %copy-start.91 = (f32[8192]{0:T(1024)}, f32[8192]{0:T(1024)S(1)}, u32[]{:S(2)}) copy-start(f32[8192]{0:T(1024)S(1)} %get-tuple-element.231) | copy-start | bytes 98308
  175.5 18.0 %all-to-all-start.2 = ((bf16[16,64,512]{2,0,1:T(8,128)(2,1)}), bf16[16,64,512]{2,0,1:T(8,128)(2,1)S(1)}, u32[]{:S(2)}, u32[]{:S(2)}) async-start(bf16[16,64,512]{2,0,1:T(8,128)(2,1)} %copy.79), calls=%async_computation.2 | async-start | bytes 2097152 | tf_op jit(solution)/shard_map/all_to_all | solution.py:89
  217.0 9.6 %all-to-all-start.3 = ((bf16[32,2,128]{2,1,0:T(2,128)(2,1)}), bf16[32,2,128]{2,1,0:T(2,128)(2,1)S(1)}, u32[]{:S(2)}, u32[]{:S(2)}) async-start(bf16[32,2,128]{2,1,0:T(2,128)(2,1)} %reshape.25776), calls=%async_computation.3 | async-start | bytes 32768 | tf_op jit(solution)/shard_map/all_to_all | solution.py:97
  (62 other events, 232.2 us)
where the time goes:
time: 229 us; the launch traced here: 227 us
  other arithmetic  62.4 us (27%)
  blocking collectives  51.6 us (23%)
  local copies, waits for them, and re-layouts  44.4 us (19%)
  waiting for transfers between devices  28.6 us (12%)
  matrix products  20.3 us (9%)
  starting transfers between devices  17.1 us (7%)
  between operations  2.58 us (1%)
    all_gather x1, blocking collectives, body(): values_piece = lax.all_gather(line_values, 'gx', axis=1, tiled=True)  30.9 us
    scatter-add x8, other arithmetic, one_source(): dense = jnp.zeros((layers, cell_count), jnp.float32).at[:, block_columns]...  26.2 us
    all_gather x1, blocking collectives, body(): columns_piece = lax.all_gather(line_columns, 'gx', axis=1, tiled=True)  20.7 us
    div x30, other arithmetic, vertical_solve(): ratios.append(-upper_coef / denominator)  20.6 us
    scatter-add x8, local copies, waits for them, and re-layouts, one_source(): dense = jnp.zeros((layers, cell_count), jnp.float32).at[:, block_columns]...  20.5 us
    dot_general x8, matrix products, one_source(): jnp.einsum('tkjn,tnm->tkjm', dense, kernel_rows, preferred_element_type=j...  19.9 us
    all_to_all x1, waiting for transfers between devices, body(): lax.all_to_all(along_x, 'gy', split_axis=0, concat_axis=1, tiled=True)  11.7 us
    all_to_all x1, waiting for transfers between devices, body(): lax.all_to_all(product, 'gy', split_axis=1, concat_axis=0, tiled=True)  11 us
  transfers between devices with their start and end apart: 4, of which 3 were waited for; matrix products, arithmetic and copies ran while one was open for 12% of the time, Pallas kernels for 0%

commit v1 on v0

--- a/solution.py
+++ b/solution.py
@@ -1,9 +1,17 @@
+import functools
 import jax
 import jax.numpy as jnp
 from jax import lax
+from jax.experimental import pallas as pl
+from jax.experimental.pallas import tpu as pltpu
 from jax.sharding import PartitionSpec as P
 
 LEV = 32
+LANES = 128
+TILE = 16
+MESH = pl.DeviceIdType.MESH
+F32 = jnp.float32
+BF16 = jnp.bfloat16
 
 
 def vertical_solve(rhs_field, coupling):
@@ -28,7 +36,7 @@
     return jnp.stack(solution[::-1], axis=1)
 
 
-def body(
+def body_exchange(
     innovations, station_columns, profile_counts, land_mask, vertical_coef, inverse_x, inverse_y
 ):
     layers = innovations.shape[1]
@@ -106,6 +114,367 @@
     return (increment, equivalents)
 
 
+def iota(shape, dim):
+    return lax.broadcasted_iota(jnp.int32, shape, dim)
+
+
+def onehot(condition):
+    return jnp.where(condition, 1.0, 0.0).astype(BF16)
+
+
+def dot(a, b):
+    return jnp.dot(a, b, preferred_element_type=F32)
+
+
+def gather_kernel(
+    dims, capacity, innov_ref, counts_ref, columns_ref, mask_ref, out_ref, mine, send_sem, recv_sem
+):
+    gx_outer, gx_inner, gy_outer, gy_inner = dims
+    gx, gy = lax.axis_index("gx"), lax.axis_index("gy")
+    i0, i1 = gx // gx_inner, lax.rem(gx, gx_inner)
+    i2, i3 = gy // gy_inner, lax.rem(gy, gy_inner)
+    far = [(lax.rem(i0 + k, gx_outer) * gx_inner + i1, gy) for k in range(1, gx_outer)]
+    across = (i0 * gx_inner + (1 - i1), gy)
+    along = (gx, (1 - i2) * gy_inner + i3)
+    twin = (gx, i2 * gy_inner + (1 - i3))
+    barrier = pltpu.get_barrier_semaphore()
+    partners = far + [across, along, twin]
+    for partner in partners:
+        pl.semaphore_signal(barrier, inc=1, device_id=partner, device_id_type=MESH)
+
+    layers, slots = innov_ref.shape
+    devices = counts_ref.shape[1]
+    cells_y, cells_x = mask_ref.shape
+    counts = jnp.broadcast_to(counts_ref[...].astype(F32), (8, devices)).astype(BF16)
+    lane_count = dot(
+        counts, onehot(iota((devices, slots), 0) == iota((devices, slots), 1) // capacity)
+    )[0:1]
+    live = lax.rem(iota((1, slots), 1), capacity).astype(F32) < lane_count
+    values = jnp.where(live, innov_ref[...].astype(F32), 0.0)
+    half = slots // 2
+    packed = jnp.concatenate([values, pltpu.roll(values, half, 1)], axis=0).T
+    mine[0:half] = packed[0:half].astype(BF16)
+    columns = columns_ref[...]
+    cell_i = lax.rem(columns, cells_x)
+    cell_j = columns // cells_x
+    at_i = onehot(iota((cells_x, slots), 0) == cell_i)
+    masks = dot(mask_ref[...].astype(F32).astype(BF16), at_i)
+    sea = jnp.sum(jnp.where(iota((cells_y, slots), 0) == cell_j, masks, 0.0), 0, keepdims=True)
+    kinds = [jnp.where(sea > 0.0, cell_i // 2, -cells_x), lax.rem(cell_i, 2), cell_j]
+    per_row = LANES // TILE
+    l_in = iota((slots, LANES), 0)
+    l_out = iota((slots, LANES), 1)
+    info = jnp.zeros((TILE, LANES), F32)
+    in_row = iota((TILE, slots), 0) == iota((TILE, slots), 1) // (capacity * per_row)
+    for kind, value in enumerate(kinds):
+        spread = (
+            (l_out // TILE == lax.rem(l_in // capacity, per_row))
+            & (lax.rem(l_out, capacity) == lax.rem(l_in, capacity))
+            & (lax.rem(l_out, TILE) // capacity == kind)
+        )
+        info += dot(jnp.where(in_row, value.astype(F32), 0.0).astype(BF16), onehot(spread))
+    mine[half : half + TILE] = info.astype(BF16)
+    out_ref[i0, i1, i2, i3] = mine[...]
+
+    pl.semaphore_wait(barrier, len(partners))
+    copies = []
+    for k, partner in enumerate(far):
+        copy = pltpu.make_async_remote_copy(
+            src_ref=mine,
+            dst_ref=out_ref.at[i0, i1, i2, i3],
+            send_sem=send_sem.at[k],
+            recv_sem=recv_sem.at[k],
+            device_id=partner,
+            device_id_type=MESH,
+        )
+        copy.start()
+        copies.append(copy)
+    for copy in copies:
+        copy.wait_recv()
+    stages = [
+        (out_ref.at[:, i1, i2, i3], across),
+        (out_ref.at[:, :, i2, i3], along),
+        (out_ref.at[:, :, :, i3], twin),
+    ]
+    for k, (block, partner) in enumerate(stages):
+        copy = pltpu.make_async_remote_copy(
+            src_ref=block,
+            dst_ref=block,
+            send_sem=send_sem.at[len(far) + k],
+            recv_sem=recv_sem.at[len(far) + k],
+            device_id=partner,
+            device_id_type=MESH,
+        )
+        copy.start()
+        copy.wait_recv()
+        copies.append(copy)
+    for copy in copies:
+        copy.wait_send()
+
+
+def field_kernel(
+    capacity,
+    all_ref,
+    kernel_x_ref,
+    kernel_y_ref,
+    coef_ref,
+    mask_ref,
+    columns_ref,
+    inc_ref,
+    picked_ref,
+    acc,
+    inverse,
+    left,
+    turned,
+):
+    block = pl.program_id(0)
+    blocks = pl.num_programs(0)
+    devices, _, _ = all_ref.shape
+    tracers, cells_x, _ = kernel_x_ref.shape
+    _, cells_y, rows_j = kernel_y_ref.shape
+    levels = coef_ref.shape[0]
+    layers = tracers * levels
+    devices_y = devices // blocks
+    per_block = devices_y * capacity
+    profiles = devices * per_block
+    per_row = LANES // TILE
+
+    @pl.when(block == 0)
+    def _():
+        acc[...] = jnp.zeros_like(acc)
+        ratio = None
+        for k in range(levels):
+            diagonal = 1.0 + coef_ref[k]
+            if k + 1 < levels:
+                diagonal += coef_ref[k + 1]
+            if k > 0:
+                diagonal += coef_ref[k] * ratio
+            inv = 1.0 / diagonal
+            inverse[k] = inv
+            if k + 1 < levels:
+                ratio = -coef_ref[k + 1] * inv
+
+    shape = (profiles, devices_y * TILE)
+    p, q = iota(shape, 0), iota(shape, 1)
+    owner = lax.rem(p // capacity, devices_y)
+    repeat = onehot(q == owner * TILE + p // (per_block * per_row))
+    info = all_ref[pl.ds(block * devices_y, devices_y), layers : layers + TILE, :]
+    info = dot(repeat, info.reshape(devices_y * TILE, LANES))
+    shape = (profiles, LANES)
+    p, q = iota(shape, 0), iota(shape, 1)
+    own = (q // TILE == lax.rem(p // per_block, per_row)) & (
+        lax.rem(q, capacity) == lax.rem(p, capacity)
+    )
+    info = jnp.where(own, info, 0.0).astype(BF16)
+    shape = (LANES, cells_x + LANES)
+    kind, n = lax.rem(iota(shape, 0), TILE) // capacity, iota(shape, 1)
+    weight = jnp.where(
+        n < cells_x,
+        jnp.where(kind == 0, 2.0, jnp.where(kind == 1, 1.0, 0.0)),
+        jnp.where(kind == 2, 1.0, 0.0),
+    ).astype(BF16)
+    place = dot(info, weight).astype(jnp.int32)
+    at_i = onehot(place[:, :cells_x] == iota((profiles, cells_x), 1))
+    p, q = iota((profiles, LANES), 0), iota((profiles, LANES), 1)
+    at_j = onehot(place[:, cells_x:] + lax.rem(p // capacity, devices_y) * cells_y == q)[:, :rows_j]
+
+    pieces = layers // per_block
+    piece = lax.rem(block, pieces)
+    part = all_ref[:, pl.ds(pl.multiple_of(piece * per_block, per_block), per_block), :]
+    turned[...] = part.reshape(profiles, LANES).astype(F32).T
+    values = turned[pl.ds(pl.multiple_of(block // pieces * layers, layers), layers), :]
+
+    for t in range(tracers):
+        smooth_y = lax.dot_general(
+            kernel_y_ref[t], at_j, (((1,), (1,)), ((), ())), preferred_element_type=F32
+        )
+        for k in range(levels):
+            r = t * levels + k
+            left[t, k * cells_y : (k + 1) * cells_y, :] = (
+                smooth_y * values[r : r + 1, :]
+            ).astype(BF16)
+        right = dot(at_i, kernel_x_ref[t]).astype(BF16)
+        acc[t] += dot(left[t], right)
+
+    @pl.when(block == blocks - 1)
+    def _():
+        mask = mask_ref[...].astype(F32)
+        for t in range(tracers):
+            carried = None
+            for k in range(levels):
+                rows = slice(k * cells_y, (k + 1) * cells_y)
+                value = acc[t, rows, :]
+                if k > 0:
+                    value += coef_ref[k] * carried
+                carried = value * inverse[k]
+                acc[t, rows, :] = carried
+            for k in range(levels - 1, -1, -1):
+                if k + 1 < levels:
+                    rows = slice(k * cells_y, (k + 1) * cells_y)
+                    carried = acc[t, rows, :] + coef_ref[k + 1] * inverse[k] * carried
+                inc_ref[t * levels + k] = (carried * mask).astype(BF16)
+        columns = columns_ref[...]
+        slots = columns.shape[1]
+        at_own = onehot(iota((cells_x, slots), 0) == lax.rem(columns, cells_x))
+        field = inc_ref[...].reshape(layers * cells_y, cells_x)
+        found = dot(field, at_own).reshape(layers, cells_y, slots)
+        in_row = iota((1, cells_y, slots), 1) == (columns // cells_x)[None]
+        picked_ref[...] = jnp.sum(jnp.where(in_row, found, 0.0), axis=1)
+
+
+def return_kernel(
+    capacity, picked_ref, counts_ref, out_ref, outgoing, arrived, rows, send_sem, recv_sem
+):
+    gx, gy = lax.axis_index("gx"), lax.axis_index("gy")
+    n_gy = lax.axis_size("gy")
+    layers, slots = picked_ref.shape
+    devices = counts_ref.shape[1]
+    me = gx * n_gy + gy
+    others = [lax.rem(me + k, devices) for k in range(1, devices)]
+    places = [(other // n_gy, lax.rem(other, n_gy)) for other in others]
+    barrier = pltpu.get_barrier_semaphore()
+    for place in places:
+        pl.semaphore_signal(barrier, inc=1, device_id=place, device_id_type=MESH)
+    picked = picked_ref[...]
+    turned = jnp.concatenate([picked, jnp.zeros((slots - layers, slots), F32)], axis=0).T
+    for d in range(devices):
+        outgoing[d] = turned[d * capacity : (d + 1) * capacity]
+    arrived[me] = outgoing[me]
+    pl.semaphore_wait(barrier, devices - 1)
+    copies = []
+    for k, (other, place) in enumerate(zip(others, places)):
+        copy = pltpu.make_async_remote_copy(
+            src_ref=outgoing.at[other],
+            dst_ref=arrived.at[me],
+            send_sem=send_sem.at[k],
+            recv_sem=recv_sem.at[k],
+            device_id=place,
+            device_id_type=MESH,
+        )
+        copy.start()
+        copies.append(copy)
+    for copy in copies:
+        copy.wait_recv()
+    for d in range(devices):
+        rows[d * capacity : (d + 1) * capacity] = arrived[d]
+    counts = jnp.broadcast_to(counts_ref[...].astype(F32), (8, devices)).astype(BF16)
+    lane_count = dot(
+        counts, onehot(iota((devices, slots), 0) == iota((devices, slots), 1) // capacity)
+    )[0:1]
+    live = lax.rem(iota((1, slots), 1), capacity).astype(F32) < lane_count
+    out_ref[...] = jnp.where(live, rows[...].T[:layers], 0.0).astype(BF16)
+    for copy in copies:
+        copy.wait_send()
+
+
+def body_gather(
+    dims,
+    innovations,
+    station_columns,
+    profile_counts,
+    land_mask,
+    vertical_coef,
+    inverse_x,
+    inverse_y,
+):
+    layers, slots = innovations.shape[1:]
+    devices = profile_counts.shape[1]
+    devices_x, devices_y = lax.axis_size("gx"), lax.axis_size("gy")
+    capacity = slots // devices
+    cells_y, cells_x = land_mask.shape
+    tracers = inverse_x.shape[0]
+    levels = layers // tracers
+    vmem = pl.BlockSpec(memory_space=pltpu.VMEM)
+    n_copies = dims[0] - 1 + 3
+    height = slots // 2 + TILE
+    gathered = pl.pallas_call(
+        functools.partial(gather_kernel, dims, capacity),
+        out_shape=jax.ShapeDtypeStruct(dims + (height, LANES), BF16),
+        in_specs=[vmem] * 4,
+        out_specs=vmem,
+        scratch_shapes=[
+            pltpu.VMEM((height, LANES), BF16),
+            pltpu.SemaphoreType.DMA((n_copies,)),
+            pltpu.SemaphoreType.DMA((n_copies,)),
+        ],
+        compiler_params=pltpu.CompilerParams(
+            collective_id=0, has_side_effects=True, vmem_limit_bytes=16 << 20
+        ),
+        name="gather_profiles",
+    )(innovations[0], profile_counts, station_columns, land_mask)
+    gathered = gathered.reshape(devices, height, LANES)
+    own_y = lax.dynamic_slice_in_dim(inverse_y, lax.axis_index("gy") * cells_y, cells_y, 2)
+    own_y = jnp.swapaxes(own_y, 1, 2)
+    profiles = devices * devices_y * capacity
+    rows = levels * cells_y
+
+    def whole(*shape):
+        return pl.BlockSpec(shape, lambda a: (0,) * len(shape))
+
+    increment, picked = pl.pallas_call(
+        functools.partial(field_kernel, capacity),
+        grid=(devices_x,),
+        out_shape=(
+            jax.ShapeDtypeStruct((layers, cells_y, cells_x), BF16),
+            jax.ShapeDtypeStruct((layers, slots), F32),
+        ),
+        in_specs=[
+            whole(devices, height, LANES),
+            pl.BlockSpec((tracers, cells_x, cells_x), lambda a: (0, a, 0)),
+            whole(*own_y.shape),
+            whole(levels, cells_y, cells_x),
+            whole(cells_y, cells_x),
+            whole(1, slots),
+        ],
+        out_specs=(whole(layers, cells_y, cells_x), whole(layers, slots)),
+        scratch_shapes=[
+            pltpu.VMEM((tracers, rows, cells_x), F32),
+            pltpu.VMEM((levels, cells_y, cells_x), F32),
+            pltpu.VMEM((tracers, rows, profiles), BF16),
+            pltpu.VMEM((LANES, profiles), F32),
+        ],
+        compiler_params=pltpu.CompilerParams(vmem_limit_bytes=40 << 20),
+        name="smooth_and_solve",
+    )(gathered, inverse_x, own_y, vertical_coef, land_mask, station_columns)
+    equivalents = pl.pallas_call(
+        functools.partial(return_kernel, capacity),
+        out_shape=jax.ShapeDtypeStruct((layers, slots), BF16),
+        in_specs=[vmem] * 2,
+        out_specs=vmem,
+        scratch_shapes=[
+            pltpu.VMEM((devices, capacity, LANES), F32),
+            pltpu.VMEM((devices, capacity, LANES), F32),
+            pltpu.VMEM((slots, LANES), F32),
+            pltpu.SemaphoreType.DMA((devices - 1,)),
+            pltpu.SemaphoreType.DMA((devices - 1,)),
+        ],
+        compiler_params=pltpu.CompilerParams(
+            collective_id=1, has_side_effects=True, vmem_limit_bytes=16 << 20
+        ),
+        name="return_equivalents",
+    )(picked, profile_counts)
+    return increment, equivalents[None]
+
+
+def plan(devices_x, devices_y, innovations, land_mask, inverse_x, inverse_y):
+    devices = devices_x * devices_y
+    layers, slots = innovations.shape[1:]
+    capacity = slots // devices
+    cells_x = land_mask.shape[1] // devices_x
+    fits = (
+        slots == LANES
+        and 2 * layers == LANES
+        and capacity * devices_y == TILE
+        and 3 * capacity <= TILE
+        and devices_x % 2 == 0
+        and devices_y == 4
+        and cells_x % LANES == 0
+        and cells_x <= 512
+        and inverse_y.shape[1] <= LANES
+    )
+    return (devices_x // 2, 2, devices_y // 2, 2) if fits else None
+
+
 def solution(mesh):
     in_specs = (
         P(("gx", "gy"), None, None),
@@ -117,4 +486,14 @@
         P(),
     )
     out_specs = (P(None, "gy", "gx"), P(("gx", "gy"), None, None))
-    return jax.shard_map(body, mesh=mesh, in_specs=in_specs, out_specs=out_specs, check_vma=False)
+
+    def run(innovations, columns, counts, land_mask, coef, inverse_x, inverse_y):
+        dims = plan(
+            mesh.shape["gx"], mesh.shape["gy"], innovations, land_mask, inverse_x, inverse_y
+        )
+        body = body_exchange if dims is None else functools.partial(body_gather, dims)
+        return jax.shard_map(
+            body, mesh=mesh, in_specs=in_specs, out_specs=out_specs, check_vma=False
+        )(innovations, columns, counts, land_mask, coef, inverse_x, inverse_y)
+
+    return run

time: 229 us -> 56.6 us (0.25)
  other arithmetic: 62.4 us -> 0 us
  blocking collectives: 51.6 us -> 0 us
  Pallas kernels: 0 us -> 45.1 us
  local copies, waits for them, and re-layouts: 44.4 us -> 10.3 us
  waiting for transfers between devices: 28.6 us -> 0 us
  matrix products: 20.3 us -> 0 us
  starting transfers between devices: 17.1 us -> 0 us
    all_gather x2 -> x0, blocking collectives: 51.6 us -> none  [the longest x1 30.9 us: body(): values_piece = lax.all_gather(line_values, 'gx', axis=1, tiled=True)]
    pallas_call x0 -> x3, Pallas kernels: none -> 45.1 us  [the longest x1 18.6 us: body_gather(): pl.pallas_call(functools.partial(field_kernel, capacity), grid=(devices_x...]
    all_to_all x4 -> x0, waiting for transfers between devices: 28.6 us -> none  [the longest x1 11.7 us: body(): lax.all_to_all(along_x, 'gy', split_axis=0, concat_axis=1, tiled=True)]
    scatter-add x8 -> x0, other arithmetic: 26.2 us -> none  [one_source(): dense = jnp.zeros((layers, cell_count), jnp.float32).at[:, block_columns]...]
    div x31 -> x0, other arithmetic: 25.6 us -> none  [the longest x30 20.6 us: vertical_solve(): ratios.append(-upper_coef / denominator)]
    scatter-add x8 -> x0, local copies, waits for them, and re-layouts: 20.5 us -> none  [one_source(): dense = jnp.zeros((layers, cell_count), jnp.float32).at[:, block_columns]...]
    dot_general x9 -> x0, matrix products: 20.3 us -> none  [the longest x8 19.9 us: one_source(): jnp.einsum('tkjn,tnm->tkjm', dense, kernel_rows, preferred_element_type=j...]
    all_to_all x4 -> x0, starting transfers between devices: 17.1 us -> none  [the longest x1 7.3 us: body(): lax.all_to_all(outgoing.reshape(layers, 1, devices_all, capacity), ('gx',...]
  transfers between devices with their start and end apart: 4 -> 0, of which waited for: 3 -> 0; matrix products, arithmetic and copies ran while one was open for 12% -> 0% of each run, Pallas kernels for 0% -> 0%
where the time goes in v1:
time: 56.6 us; the launch traced here: 56.1 us
  Pallas kernels  45.1 us (80%)
  local copies, waits for them, and re-layouts  10.3 us (18%)
  between operations  0.69 us (1%)
    pallas_call x1, Pallas kernels, body_gather(): pl.pallas_call(functools.partial(field_kernel, capacity), grid=(devices_x...  18.6 us
    pallas_call x1, Pallas kernels, body_gather(): pl.pallas_call(functools.partial(gather_kernel, dims, capacity), out_shap...  17.9 us
    unnamed x22, local copies, waits for them, and re-layouts  10.2 us
    pallas_call x1, Pallas kernels, body_gather(): pl.pallas_call(functools.partial(return_kernel, capacity), out_shape=jax....  8.57 us

profile of v1, /device:TPU:0, one launch (start us, length us, event | category | flops | bytes accessed | tf_op | source)
XLA Modules:
  0.0 56.1 jit_solution(7343718155407797865)
XLA Ops:
  0.6 0.0 copy-start
  0.6 0.0 copy-start.9
  0.7 0.7 %copy-done = bf16[2,64,64]{2,1,0:T(8,128)(2,1)S(1)} copy-done((bf16[2,64,64]{2,1,0:T(8,128)(2,1)S(1)}, bf16[2,64,64]{2,1,0:T(8,128)(2,1)}, u32[]{:S(2)}) %copy-start) | copy-done | bytes 16408
  1.4 0.1 constant_dynamic-slice_fusion
  1.5 0.1 copy.10
  1.6 0.0 copy-start.3
  1.6 0.8 %copy-done.3 = s32[16,512]{1,0:T(8,128)S(1)} copy-done((s32[16,512]{1,0:T(8,128)S(1)}, s32[16,512]{1,0:T(8,128)}, u32[]{:S(2)}) %copy-start.3) | copy-done | bytes 32792
  2.3 0.0 copy-start.5
  2.3 0.7 %copy-done.5 = bf16[1,64,128]{2,1,0:T(8,128)(2,1)S(1)} copy-done((bf16[1,64,128]{2,1,0:T(8,128)(2,1)S(1)}, bf16[1,64,128]{2,1,0:T(8,128)(2,1)}, u32[]{:S(2)}) %copy-start.5) | copy-done | bytes 16408
  3.0 0.0 copy-start.6
  3.0 0.7 %copy-done.6 = s32[1,128]{1,0:T(1,128)S(1)} copy-done((s32[1,128]{1,0:T(1,128)S(1)}, s32[1,128]{1,0:T(1,128)}, u32[]{:S(2)}) %copy-start.6) | copy-done | bytes 536
  3.7 0.0 copy-start.8
  3.7 0.7 %copy-done.8 = s32[1,32]{1,0:T(1,128)S(1)} copy-done((s32[1,32]{1,0:T(1,128)S(1)}, s32[1,32]{1,0:T(1,128)}, u32[]{:S(2)}) %copy-start.8) | copy-done | bytes 152
  4.4 17.9 %gather_profiles.1 = bf16[4,2,2,2,80,128]{5,4,3,2,1,0:T(8,128)(2,1)S(1)} custom-call(bf16[64,128]{1,0:T(8,128)(2,1)S(1)} %bitcast.7, s32[1,32]{1,0:T(1,128)S(1)} %copy-done.8, s32[1,128]{1,0:T(1,128)S(1)} %copy-done.6, s32[16,512]{1,0:T(8,128)S(1)} %copy-done.3), custom_call_target="tpu_custom_call" | custom-call | tf_op jit(solution)/shard_map/gather_profiles/pallas_call | solution.py:390
  22.2 0.0 copy-start.1
  22.2 3.4 %copy-done.1 = bf16[2,4096,512]{2,1,0:T(8,128)(2,1)S(1)} copy-done((bf16[2,4096,512]{2,1,0:T(8,128)(2,1)S(1)}, bf16[2,4096,512]{2,1,0:T(8,128)(2,1)}, u32[]{:S(2)}) %copy-start.1) | copy-done | bytes 8388632
  25.6 0.0 copy-start.2
  25.6 1.2 %copy-done.2 = f32[32,16,512]{2,1,0:T(8,128)S(1)} copy-done((f32[32,16,512]{2,1,0:T(8,128)S(1)}, f32[32,16,512]{2,1,0:T(8,128)}, u32[]{:S(2)}) %copy-start.2) | copy-done | bytes 1048600
  26.8 0.0 copy-start.4
  26.8 0.8 %copy-done.4 = s32[16,512]{1,0:T(8,128)S(1)} copy-done((s32[16,512]{1,0:T(8,128)S(1)}, s32[16,512]{1,0:T(8,128)}, u32[]{:S(2)}) %copy-start.4) | copy-done | bytes 32792
  27.6 0.0 copy-start.7
  27.6 0.7 %copy-done.7 = s32[1,128]{1,0:T(1,128)S(1)} copy-done((s32[1,128]{1,0:T(1,128)S(1)}, s32[1,128]{1,0:T(1,128)}, u32[]{:S(2)}) %copy-start.7) | copy-done | bytes 536
  28.3 18.6 %smooth_and_solve.1 = (bf16[64,16,512]{2,1,0:T(8,128)(2,1)}, f32[64,128]{1,0:T(8,128)S(1)}) custom-call(bf16[32,80,128]{2,1,0:T(8,128)(2,1)S(1)} %bitcast.4, bf16[2,4096,512]{2,1,0:T(8,128)(2,1)S(1)} %copy-done.1, bf16[2,16,64]{2,1,0:T(8,128)(2,1)S(1)} %bitcast.6, f32[32,16,512]{2,1,0:T(8,128)S(1)} %copy-done.2, s32[16,512]{1,0:T(8,128)S(1)} %copy-done.4, ...), custom_call_target="tpu_custom_call" | custom-call | tf_op jit(solution)/shard_map/smooth_and_solve/pallas_call | solution.py:414
  46.9 0.0 copy-done.9
  46.9 8.6 %return_equivalents.1 = bf16[64,128]{1,0:T(8,128)(2,1)S(1)} custom-call(f32[64,128]{1,0:T(8,128)S(1)} %get-tuple-element.5.picked_ref, s32[1,32]{1,0:T(1,128)S(1)} %copy-done.9), custom_call_target="tpu_custom_call" | custom-call | tf_op jit(solution)/shard_map/return_equivalents/pallas_call | solution.py:439
  55.5 0.6 %copy.12 = bf16[1,64,128]{2,1,0:T(8,128)(2,1)} copy(bf16[1,64,128]{2,1,0:T(8,128)(2,1)S(1)} %bitcast.5) | data formatting | bytes 32768
Async XLA Ops:
  0.6 0.8 %copy-start = (bf16[2,64,64]{2,1,0:T(8,128)(2,1)S(1)}, bf16[2,64,64]{2,1,0:T(8,128)(2,1)}, u32[]{:S(2)}) copy-start(bf16[2,64,64]{2,1,0:T(8,128)(2,1)} %param.13) | copy-start | bytes 49156
  0.6 46.3 %copy-start.9 = (s32[1,32]{1,0:T(1,128)S(1)}, s32[1,32]{1,0:T(1,128)}, u32[]{:S(2)}) copy-start(s32[1,32]{1,0:T(1,128)} %counts_ref.3) | copy-start | bytes 388
  1.6 0.8 %copy-start.3 = (s32[16,512]{1,0:T(8,128)S(1)}, s32[16,512]{1,0:T(8,128)}, u32[]{:S(2)}) copy-start(s32[16,512]{1,0:T(8,128)} %mask_ref.3) | copy-start | bytes 98308
  2.3 0.7 %copy-start.5 = (bf16[1,64,128]{2,1,0:T(8,128)(2,1)S(1)}, bf16[1,64,128]{2,1,0:T(8,128)(2,1)}, u32[]{:S(2)}) copy-start(bf16[1,64,128]{2,1,0:T(8,128)(2,1)} %param.7) | copy-start | bytes 49156
  3.0 0.7 %copy-start.6 = (s32[1,128]{1,0:T(1,128)S(1)}, s32[1,128]{1,0:T(1,128)}, u32[]{:S(2)}) copy-start(s32[1,128]{1,0:T(1,128)} %columns_ref.3) | copy-start | bytes 1540
  3.7 0.7 %copy-start.8 = (s32[1,32]{1,0:T(1,128)S(1)}, s32[1,32]{1,0:T(1,128)}, u32[]{:S(2)}) copy-start(s32[1,32]{1,0:T(1,128)} %counts_ref.3) | copy-start | bytes 388
  22.2 3.4 %copy-start.1 = (bf16[2,4096,512]{2,1,0:T(8,128)(2,1)S(1)}, bf16[2,4096,512]{2,1,0:T(8,128)(2,1)}, u32[]{:S(2)}) copy-start(bf16[2,4096,512]{2,1,0:T(8,128)(2,1)} %kernel_x_ref.1) | copy-start | bytes 25165828
  25.6 1.2 %copy-start.2 = (f32[32,16,512]{2,1,0:T(8,128)S(1)}, f32[32,16,512]{2,1,0:T(8,128)}, u32[]{:S(2)}) copy-start(f32[32,16,512]{2,1,0:T(8,128)} %coef_ref.1) | copy-start | bytes 3145732
  26.8 0.8 %copy-start.4 = (s32[16,512]{1,0:T(8,128)S(1)}, s32[16,512]{1,0:T(8,128)}, u32[]{:S(2)}) copy-start(s32[16,512]{1,0:T(8,128)} %mask_ref.3) | copy-start | bytes 98308
  27.6 0.7 %copy-start.7 = (s32[1,128]{1,0:T(1,128)S(1)}, s32[1,128]{1,0:T(1,128)}, u32[]{:S(2)}) copy-start(s32[1,128]{1,0:T(1,128)} %columns_ref.3) | copy-start | bytes 1540

commit v2 on v0

--- a/solution.py
+++ b/solution.py
@@ -1,9 +1,18 @@
+import functools
 import jax
 import jax.numpy as jnp
 from jax import lax
+from jax.experimental import pallas as pl
+from jax.experimental.pallas import tpu as pltpu
 from jax.sharding import PartitionSpec as P
 
 LEV = 32
+LANES = 128
+TILE = 16
+VMEM_BYTES = 56 << 20
+MESH = pl.DeviceIdType.MESH
+F32 = jnp.float32
+BF16 = jnp.bfloat16
 
 
 def vertical_solve(rhs_field, coupling):
@@ -28,7 +37,7 @@
     return jnp.stack(solution[::-1], axis=1)
 
 
-def body(
+def body_exchange(
     innovations, station_columns, profile_counts, land_mask, vertical_coef, inverse_x, inverse_y
 ):
     layers = innovations.shape[1]
@@ -106,6 +115,412 @@
     return (increment, equivalents)
 
 
+def iota(shape, dim):
+    return lax.broadcasted_iota(jnp.int32, shape, dim)
+
+
+def onehot(condition):
+    return jnp.where(condition, 1.0, 0.0).astype(BF16)
+
+
+def dot(a, b):
+    return jnp.dot(a, b, preferred_element_type=F32)
+
+
+def profile_kernel(
+    dims,
+    capacity,
+    innov_hbm,
+    columns_hbm,
+    counts_hbm,
+    mask_hbm,
+    coef_hbm,
+    kernel_x_hbm,
+    kernel_y_hbm,
+    inc_hbm,
+    equiv_hbm,
+    innov_ref,
+    columns_ref,
+    counts_ref,
+    mask_ref,
+    coef_ref,
+    kernel_x_ref,
+    kernel_y_ref,
+    cells,
+    profiles,
+    smooth_y,
+    left,
+    turned,
+    acc,
+    inverse,
+    ratio,
+    inc_ref,
+    outgoing,
+    arrived,
+    rows,
+    equiv_ref,
+    load_sem,
+    store_sem,
+    cell_send,
+    cell_recv,
+    prof_send,
+    prof_recv,
+    back_send,
+    back_recv,
+):
+    gx_outer, gx_inner, gy_outer, gy_inner = dims
+    blocks, devices_y = gx_outer * gx_inner, gy_outer * gy_inner
+    gx, gy = lax.axis_index("gx"), lax.axis_index("gy")
+    i0, i1 = gx // gx_inner, lax.rem(gx, gx_inner)
+    i2, i3 = gy // gy_inner, lax.rem(gy, gy_inner)
+    me = gx * devices_y + gy
+    layers, slots = innov_ref.shape
+    devices = blocks * devices_y
+    levels, cells_y, cells_x = coef_ref.shape
+    tracers, rows_j, _ = kernel_y_ref.shape
+    per_block = devices_y * capacity
+    count = devices * per_block
+
+    loads = [
+        pltpu.make_async_copy(source, target, load_sem.at[k])
+        for k, (source, target) in enumerate(
+            [
+                (columns_hbm, columns_ref),
+                (mask_hbm, mask_ref),
+                (counts_hbm, counts_ref),
+                (innov_hbm, innov_ref),
+                (coef_hbm, coef_ref),
+                (kernel_y_hbm, kernel_y_ref),
+                (kernel_x_hbm, kernel_x_ref),
+            ]
+        )
+    ]
+    for load in loads:
+        load.start()
+
+    def place(k):
+        other = lax.rem(me + k, devices)
+        return other, (other // devices_y, lax.rem(other, devices_y))
+
+    barrier = pltpu.get_barrier_semaphore()
+
+    @pl.loop(1, devices)
+    def _(k):
+        pl.semaphore_signal(barrier, inc=1, device_id=place(k)[1], device_id_type=MESH)
+
+    loads[0].wait()
+    loads[1].wait()
+    columns = columns_ref[...]
+    cell_i, cell_j = columns & (cells_x - 1), columns // cells_x
+    at_own = onehot(iota((cells_x, slots), 0) == cell_i)
+    masks = dot(mask_ref[...].astype(F32).astype(BF16), at_own)
+    sea = jnp.sum(jnp.where(iota((cells_y, slots), 0) == cell_j, masks, 0.0), 0, keepdims=True)
+    cells[me] = jnp.where(sea > 0.0, columns, -1)
+    pl.semaphore_wait(barrier, devices - 1)
+
+    def cell_copy(k):
+        return pltpu.make_async_remote_copy(
+            src_ref=cells.at[me],
+            dst_ref=cells.at[me],
+            send_sem=cell_send.at[k - 1],
+            recv_sem=cell_recv.at[k - 1],
+            device_id=place(k)[1],
+            device_id_type=MESH,
+        )
+
+    @pl.loop(1, devices)
+    def _(k):
+        cell_copy(k).start()
+
+    loads[2].wait()
+    loads[3].wait()
+    counts = jnp.broadcast_to(counts_ref[...].astype(F32), (8, devices)).astype(BF16)
+    lane_count = dot(
+        counts, onehot(iota((devices, slots), 0) == iota((devices, slots), 1) // capacity)
+    )[0:1]
+    live = (iota((1, slots), 1) & (capacity - 1)).astype(F32) < lane_count
+    values = jnp.where(live, innov_ref[...].astype(F32), 0.0)
+    half = slots // 2
+    packed = jnp.concatenate([values, pltpu.roll(values, half, 1)], axis=0).T
+    profiles[i0, i1, i2, i3] = packed[0:half].astype(BF16)
+
+    sent = []
+
+    def send(block, partner):
+        copy = pltpu.make_async_remote_copy(
+            src_ref=block,
+            dst_ref=block,
+            send_sem=prof_send.at[len(sent)],
+            recv_sem=prof_recv.at[len(sent)],
+            device_id=partner,
+            device_id_type=MESH,
+        )
+        copy.start()
+        sent.append(copy)
+        return copy
+
+    across = (i0 * gx_inner + (1 - i1), gy)
+    along = (gx, (1 - i2) * gy_inner + i3)
+    twin = (gx, i2 * gy_inner + (1 - i3))
+    far = [
+        send(
+            profiles.at[i0, i1, i2, i3],
+            (lax.rem(i0 + k, gx_outer) * gx_inner + i1, gy),
+        )
+        for k in range(1, gx_outer)
+    ]
+
+    loads[4].wait()
+    last = None
+    for k in range(levels):
+        diagonal = 1.0 + coef_ref[k]
+        if k + 1 < levels:
+            diagonal += coef_ref[k + 1]
+        if k > 0:
+            diagonal -= coef_ref[k] * last
+        inv = 1.0 / diagonal
+        inverse[k] = inv
+        if k + 1 < levels:
+            last = coef_ref[k + 1] * inv
+            ratio[k] = last
+
+    for copy in far:
+        copy.wait_recv()
+    own_line = profiles.at[:, i1, i2, i3]
+    by_x = send(own_line, across)
+    by_y = send(own_line, along)
+    to_twin = [send(own_line, twin)]
+
+    @pl.loop(1, devices)
+    def _(k):
+        cell_copy(k).wait_recv()
+
+    loads[5].wait()
+    loads[6].wait()
+    own_rows = onehot(iota((cells_y, rows_j), 1) == gy * cells_y + iota((cells_y, rows_j), 0))
+    own_y = [
+        lax.dot_general(
+            own_rows, kernel_y_ref[t], (((1,), (1,)), ((), ())), preferred_element_type=F32
+        ).astype(BF16)
+        for t in range(tracers)
+    ]
+    row = iota((per_block, slots), 0)
+    shape = (devices, per_block, slots)
+    own_lane = iota(shape, 2) == iota(shape, 0) * capacity + (iota(shape, 1) & (capacity - 1))
+    own_lane = jnp.where(own_lane, 1.0, 0.0)
+    owner = (iota((count, 1), 0) & (per_block - 1)) // capacity
+
+    def pick_rows(block):
+        tile = jnp.zeros((per_block, slots), jnp.int32)
+        for b in range(devices_y):
+            tile = jnp.where(row // capacity == b, cells[block * devices_y + b], tile)
+        cell = jnp.sum(own_lane * tile.astype(F32)[None], axis=2, keepdims=True)
+        cell = cell.reshape(count, 1).astype(jnp.int32)
+        column = jnp.where(cell < 0, -1, cell & (cells_x - 1))
+        at_i = onehot(iota((count, cells_x), 1) == column)
+        at_j = onehot(iota((count, rows_j), 1) == owner * cells_y + (cell // cells_x))
+        lines = pl.ds(pl.multiple_of(block * cells_x, cells_x), cells_x)
+        for t in range(tracers):
+            smooth_y[block, t] = lax.dot_general(
+                own_y[t], at_j, (((1,), (1,)), ((), ())), preferred_element_type=F32
+            )
+            kernel_x_ref[t, lines, :] = dot(at_i, kernel_x_ref[t, lines, :]).astype(BF16)
+
+    pl.loop(0, blocks // 4)(pick_rows)
+    by_x.wait_recv()
+    by_y.wait_recv()
+    from_x, from_y = profiles.at[:, 1 - i1, i2, i3], profiles.at[:, i1, 1 - i2, i3]
+    diagonals = [
+        send(from_x.at[:, 0 : half // 2], along),
+        send(from_y.at[:, half // 2 : half], across),
+    ]
+    to_twin += [send(from_x, twin), send(from_y, twin)]
+    pl.loop(blocks // 4, blocks // 2)(pick_rows)
+    for copy in diagonals:
+        copy.wait_recv()
+    to_twin.append(send(profiles.at[:, 1 - i1, 1 - i2, i3], twin))
+    pl.loop(blocks // 2, blocks)(pick_rows)
+    for copy in to_twin:
+        copy.wait_recv()
+
+    pieces = half // per_block
+    acc[...] = jnp.zeros_like(acc)
+
+    @pl.loop(0, blocks)
+    def _(block):
+        piece = pl.multiple_of(lax.rem(block, pieces) * per_block, per_block)
+        part = profiles[:, :, :, :, pl.ds(piece, per_block), :]
+        turned[...] = part.reshape(count, LANES).astype(F32).T
+        base = pl.multiple_of(block // pieces * layers, layers)
+        values = turned[pl.ds(base, layers), :]
+        lines = pl.ds(pl.multiple_of(block * cells_x, cells_x), cells_x)
+        for t in range(tracers):
+            weights = smooth_y[block, t]
+            for k in range(levels):
+                r = t * levels + k
+                left[t, k * cells_y : (k + 1) * cells_y, :] = (
+                    weights * values[r : r + 1, :]
+                ).astype(BF16)
+            acc[t] += dot(left[t], kernel_x_ref[t, lines, :])
+
+    mask = mask_ref[...].astype(F32)
+    carried = [None] * tracers
+    for k in range(levels):
+        lines = slice(k * cells_y, (k + 1) * cells_y)
+        for t in range(tracers):
+            value = acc[t, lines, :]
+            if k > 0:
+                value += coef_ref[k] * carried[t]
+            carried[t] = value * inverse[k]
+            acc[t, lines, :] = carried[t]
+    for k in range(levels - 1, -1, -1):
+        lines = slice(k * cells_y, (k + 1) * cells_y)
+        for t in range(tracers):
+            if k + 1 < levels:
+                carried[t] = acc[t, lines, :] + ratio[k] * carried[t]
+            inc_ref[t * levels + k] = (carried[t] * mask).astype(BF16)
+    store = pltpu.make_async_copy(inc_ref, inc_hbm, store_sem.at[0])
+    store.start()
+
+    field = inc_ref[...].reshape(layers * cells_y, cells_x)
+    found = dot(field, at_own).reshape(layers, cells_y, slots)
+    in_row = iota((1, cells_y, slots), 1) == cell_j[None]
+    picked = jnp.sum(jnp.where(in_row, found, 0.0), axis=1)
+    picked = jnp.concatenate([picked, jnp.zeros((slots - layers, slots), F32)], axis=0).T
+    for d in range(devices):
+        outgoing[d] = picked[d * capacity : (d + 1) * capacity]
+    arrived[me] = outgoing[me]
+
+    def back_copy(k):
+        other, where = place(k)
+        return pltpu.make_async_remote_copy(
+            src_ref=outgoing.at[other],
+            dst_ref=arrived.at[me],
+            send_sem=back_send.at[k - 1],
+            recv_sem=back_recv.at[k - 1],
+            device_id=where,
+            device_id_type=MESH,
+        )
+
+    @pl.loop(1, devices)
+    def _(k):
+        back_copy(k).start()
+
+    for copy in sent:
+        copy.wait_send()
+
+    @pl.loop(1, devices)
+    def _(k):
+        cell_copy(k).wait_send()
+
+    @pl.loop(1, devices)
+    def _(k):
+        back_copy(k).wait_recv()
+
+    for d in range(devices):
+        rows[d * capacity : (d + 1) * capacity] = arrived[d]
+    equiv_ref[...] = jnp.where(live, rows[...].T[:layers], 0.0).astype(BF16)
+    result = pltpu.make_async_copy(equiv_ref, equiv_hbm, store_sem.at[1])
+    result.start()
+
+    @pl.loop(1, devices)
+    def _(k):
+        back_copy(k).wait_send()
+
+    store.wait()
+    result.wait()
+
+
+def body_gather(
+    dims,
+    innovations,
+    station_columns,
+    profile_counts,
+    land_mask,
+    vertical_coef,
+    inverse_x,
+    inverse_y,
+):
+    layers, slots = innovations.shape[1:]
+    devices = profile_counts.shape[1]
+    devices_y = dims[2] * dims[3]
+    capacity = slots // devices
+    cells_y, cells_x = land_mask.shape
+    tracers = inverse_x.shape[0]
+    levels = layers // tracers
+    blocks = dims[0] * dims[1]
+    count = devices * devices_y * capacity
+    anywhere = pl.BlockSpec(memory_space=pl.ANY)
+    operands = (
+        innovations[0],
+        station_columns,
+        profile_counts,
+        land_mask,
+        vertical_coef,
+        inverse_x,
+        inverse_y,
+    )
+    n_profile = dims[0] - 1 + 8
+    increment, equivalents = pl.pallas_call(
+        functools.partial(profile_kernel, dims, capacity),
+        out_shape=(
+            jax.ShapeDtypeStruct((layers, cells_y, cells_x), BF16),
+            jax.ShapeDtypeStruct((layers, slots), BF16),
+        ),
+        in_specs=[anywhere] * len(operands),
+        out_specs=(anywhere, anywhere),
+        scratch_shapes=[pltpu.VMEM(x.shape, x.dtype) for x in operands]
+        + [
+            pltpu.VMEM((devices, 1, slots), jnp.int32),
+            pltpu.VMEM(dims + (slots // 2, LANES), BF16),
+            pltpu.VMEM((blocks, tracers, cells_y, count), F32),
+            pltpu.VMEM((tracers, levels * cells_y, count), BF16),
+            pltpu.VMEM((LANES, count), F32),
+            pltpu.VMEM((tracers, levels * cells_y, cells_x), F32),
+            pltpu.VMEM((levels, cells_y, cells_x), F32),
+            pltpu.VMEM((levels, cells_y, cells_x), F32),
+            pltpu.VMEM((layers, cells_y, cells_x), BF16),
+            pltpu.VMEM((devices, capacity, LANES), F32),
+            pltpu.VMEM((devices, capacity, LANES), F32),
+            pltpu.VMEM((slots, LANES), F32),
+            pltpu.VMEM((layers, slots), BF16),
+            pltpu.SemaphoreType.DMA((len(operands),)),
+            pltpu.SemaphoreType.DMA((2,)),
+            pltpu.SemaphoreType.DMA((devices - 1,)),
+            pltpu.SemaphoreType.DMA((devices - 1,)),
+            pltpu.SemaphoreType.DMA((n_profile,)),
+            pltpu.SemaphoreType.DMA((n_profile,)),
+            pltpu.SemaphoreType.DMA((devices - 1,)),
+            pltpu.SemaphoreType.DMA((devices - 1,)),
+        ],
+        compiler_params=pltpu.CompilerParams(
+            collective_id=0, has_side_effects=True, vmem_limit_bytes=VMEM_BYTES
+        ),
+        name="smooth_profiles",
+    )(*operands)
+    return increment, equivalents[None]
+
+
+def plan(devices_x, devices_y, innovations, land_mask, inverse_x, inverse_y):
+    devices = devices_x * devices_y
+    layers, slots = innovations.shape[1:]
+    capacity = slots // devices
+    cells_x = land_mask.shape[1] // devices_x
+    fits = (
+        slots == LANES
+        and 2 * layers == LANES
+        and capacity * devices_y == TILE
+        and devices_x % 2 == 0
+        and devices_y == 4
+        and devices_x % 4 == 0
+        and cells_x % LANES == 0
+        and cells_x & (cells_x - 1) == 0
+        and cells_x == devices * TILE
+        and inverse_y.shape[1] <= LANES
+    )
+    return (devices_x // 2, 2, devices_y // 2, 2) if fits else None
+
+
 def solution(mesh):
     in_specs = (
         P(("gx", "gy"), None, None),
@@ -117,4 +532,14 @@
         P(),
     )
     out_specs = (P(None, "gy", "gx"), P(("gx", "gy"), None, None))
-    return jax.shard_map(body, mesh=mesh, in_specs=in_specs, out_specs=out_specs, check_vma=False)
+
+    def run(innovations, columns, counts, land_mask, coef, inverse_x, inverse_y):
+        dims = plan(
+            mesh.shape["gx"], mesh.shape["gy"], innovations, land_mask, inverse_x, inverse_y
+        )
+        body = body_exchange if dims is None else functools.partial(body_gather, dims)
+        return jax.shard_map(
+            body, mesh=mesh, in_specs=in_specs, out_specs=out_specs, check_vma=False
+        )(innovations, columns, counts, land_mask, coef, inverse_x, inverse_y)
+
+    return run

time: 229 us -> 40.8 us (0.18)
  other arithmetic: 62.4 us -> 0 us
  blocking collectives: 51.6 us -> 0 us
  local copies, waits for them, and re-layouts: 44.4 us -> 3.59 us
  Pallas kernels: 0 us -> 36.3 us
  waiting for transfers between devices: 28.6 us -> 0 us
  matrix products: 20.3 us -> 0 us
  starting transfers between devices: 17.1 us -> 0 us
    all_gather x2 -> x0, blocking collectives: 51.6 us -> none  [the longest x1 30.9 us: body(): values_piece = lax.all_gather(line_values, 'gx', axis=1, tiled=True)]
    pallas_call x0 -> x1, Pallas kernels: none -> 36.3 us  [body_gather(): pl.pallas_call(functools.partial(profile_kernel, dims, capacity), out_sha...]
    all_to_all x4 -> x0, waiting for transfers between devices: 28.6 us -> none  [the longest x1 11.7 us: body(): lax.all_to_all(along_x, 'gy', split_axis=0, concat_axis=1, tiled=True)]
    scatter-add x8 -> x0, other arithmetic: 26.2 us -> none  [one_source(): dense = jnp.zeros((layers, cell_count), jnp.float32).at[:, block_columns]...]
    div x31 -> x0, other arithmetic: 25.6 us -> none  [the longest x30 20.6 us: vertical_solve(): ratios.append(-upper_coef / denominator)]
    scatter-add x8 -> x0, local copies, waits for them, and re-layouts: 20.5 us -> none  [one_source(): dense = jnp.zeros((layers, cell_count), jnp.float32).at[:, block_columns]...]
    dot_general x9 -> x0, matrix products: 20.3 us -> none  [the longest x8 19.9 us: one_source(): jnp.einsum('tkjn,tnm->tkjm', dense, kernel_rows, preferred_element_type=j...]
    all_to_all x4 -> x0, starting transfers between devices: 17.1 us -> none  [the longest x1 7.3 us: body(): lax.all_to_all(outgoing.reshape(layers, 1, devices_all, capacity), ('gx',...]
  transfers between devices with their start and end apart: 4 -> 0, of which waited for: 3 -> 0; matrix products, arithmetic and copies ran while one was open for 12% -> 0% of each run, Pallas kernels for 0% -> 0%
where the time goes in v2:
time: 40.8 us; the launch traced here: 40.6 us
  Pallas kernels  36.3 us (89%)
  local copies, waits for them, and re-layouts  3.59 us (9%)
  between operations  0.64 us (2%)
    pallas_call x1, Pallas kernels, body_gather(): pl.pallas_call(functools.partial(profile_kernel, dims, capacity), out_sha...  36.3 us
    unnamed x2, local copies, waits for them, and re-layouts  3.59 us

profile of v2, /device:TPU:0, one launch (start us, length us, event | category | flops | bytes accessed | tf_op | source)
XLA Modules:
  0.0 40.6 jit_solution(17174160262073061206)
XLA Ops:
  0.6 36.3 %smooth_profiles.1 = (bf16[64,16,512]{2,1,0:T(8,128)(2,1)}, bf16[64,128]{1,0:T(8,128)(2,1)}) custom-call(bf16[64,128]{1,0:T(8,128)(2,1)} %bitcast.2, s32[1,128]{1,0:T(1,128)} %columns_hbm.1, s32[1,32]{1,0:T(1,128)} %counts_hbm.1, s32[16,512]{1,0:T(8,128)} %mask_hbm.1, f32[32,16,512]{2,1,0:T(8,128)} %coef_hbm.1, bf16[2,4096,512]{2,1,0:T(8,128)(2,1)} %kernel_x_hbm.1, ...), custom_call_target="tpu_custom_call" | custom-call | tf_op jit(solution)/shard_map/smooth_profiles/pallas_call | solution.py:464
  37.0 2.3 %copy.11 = bf16[64,16,512]{2,1,0:T(8,128)(2,1)} copy(bf16[64,16,512]{2,1,0:T(8,128)(2,1)} %get-tuple-element.8) | data formatting | bytes 2097152
  39.2 1.3 %copy.12 = bf16[1,64,128]{2,1,0:T(8,128)(2,1)} copy(bf16[1,64,128]{2,1,0:T(8,128)(2,1)} %bitcast.3) | data formatting | bytes 32768

commit v3 on v2

--- a/solution.py
+++ b/solution.py
@@ -148,6 +148,8 @@
     kernel_y_ref,
     cells,
     profiles,
+    place_x,
+    picked_x,
     smooth_y,
     left,
     turned,
@@ -200,7 +202,7 @@
 
     def place(k):
         other = lax.rem(me + k, devices)
-        return other, (other // devices_y, lax.rem(other, devices_y))
+        return other, (lax.div(other, devices_y), lax.rem(other, devices_y))
 
     barrier = pltpu.get_barrier_semaphore()
 
@@ -307,26 +309,40 @@
     row = iota((per_block, slots), 0)
     shape = (devices, per_block, slots)
     own_lane = iota(shape, 2) == iota(shape, 0) * capacity + (iota(shape, 1) & (capacity - 1))
-    own_lane = jnp.where(own_lane, 1.0, 0.0)
-    owner = (iota((count, 1), 0) & (per_block - 1)) // capacity
-
-    def pick_rows(block):
-        tile = jnp.zeros((per_block, slots), jnp.int32)
-        for b in range(devices_y):
-            tile = jnp.where(row // capacity == b, cells[block * devices_y + b], tile)
-        cell = jnp.sum(own_lane * tile.astype(F32)[None], axis=2, keepdims=True)
-        cell = cell.reshape(count, 1).astype(jnp.int32)
-        column = jnp.where(cell < 0, -1, cell & (cells_x - 1))
-        at_i = onehot(iota((count, cells_x), 1) == column)
-        at_j = onehot(iota((count, rows_j), 1) == owner * cells_y + (cell // cells_x))
-        lines = pl.ds(pl.multiple_of(block * cells_x, cells_x), cells_x)
-        for t in range(tracers):
-            smooth_y[block, t] = lax.dot_general(
-                own_y[t], at_j, (((1,), (1,)), ((), ())), preferred_element_type=F32
+    owner = (iota((count, LANES), 0) & (per_block - 1)) // capacity
+    lane = iota((count, LANES), 1)
+    join = jnp.where(iota((2 * slots, LANES), 0) < slots, 32.0, 1.0).astype(BF16)
+
+    @pl.loop(0, blocks // 2)
+    def _(pair):
+        for block in (2 * pair, 2 * pair + 1):
+            tile = jnp.zeros((per_block, slots), jnp.int32)
+            for b in range(devices_y):
+                tile = jnp.where(row // capacity == b, cells[block * devices_y + b], tile)
+            parts = [
+                jnp.where(own_lane, part.astype(F32)[None], 0.0).reshape(count, slots).astype(BF16)
+                for part in (tile >> 5, tile & 31)
+            ]
+            cell = dot(jnp.concatenate(parts, axis=1), join).astype(jnp.int32)
+            place_x[block] = jnp.where(cell < 0, -1, cell & (cells_x - 1))
+            at_j = onehot(lane == owner * cells_y + cell // cells_x)[:, :rows_j]
+            for t in range(tracers):
+                smooth_y[block, t] = lax.dot_general(
+                    own_y[t], at_j, (((1,), (1,)), ((), ())), preferred_element_type=F32
+                )
+
+    def pick_rows(pair):
+        for block in (2 * pair, 2 * pair + 1):
+            column = place_x[block]
+            at_i = jnp.concatenate(
+                [onehot(column == lane + start) for start in range(0, cells_x, LANES)], axis=1
             )
-            kernel_x_ref[t, lines, :] = dot(at_i, kernel_x_ref[t, lines, :]).astype(BF16)
-
-    pl.loop(0, blocks // 4)(pick_rows)
+            lines = pl.ds(pl.multiple_of(block * cells_x, cells_x), cells_x)
+            target = pl.ds(pl.multiple_of(block * count, count), count)
+            for t in range(tracers):
+                picked_x[t, target, :] = dot(at_i, kernel_x_ref[t, lines, :]).astype(BF16)
+
+    pl.loop(0, 1)(pick_rows)
     by_x.wait_recv()
     by_y.wait_recv()
     from_x, from_y = profiles.at[:, 1 - i1, i2, i3], profiles.at[:, i1, 1 - i2, i3]
@@ -335,33 +351,42 @@
         send(from_y.at[:, half // 2 : half], across),
     ]
     to_twin += [send(from_x, twin), send(from_y, twin)]
-    pl.loop(blocks // 4, blocks // 2)(pick_rows)
+    pl.loop(1, 2)(pick_rows)
     for copy in diagonals:
         copy.wait_recv()
     to_twin.append(send(profiles.at[:, 1 - i1, 1 - i2, i3], twin))
-    pl.loop(blocks // 2, blocks)(pick_rows)
+    pl.loop(2, blocks // 2)(pick_rows)
     for copy in to_twin:
         copy.wait_recv()
 
     pieces = half // per_block
     acc[...] = jnp.zeros_like(acc)
-
-    @pl.loop(0, blocks)
-    def _(block):
-        piece = pl.multiple_of(lax.rem(block, pieces) * per_block, per_block)
-        part = profiles[:, :, :, :, pl.ds(piece, per_block), :]
-        turned[...] = part.reshape(count, LANES).astype(F32).T
-        base = pl.multiple_of(block // pieces * layers, layers)
-        values = turned[pl.ds(base, layers), :]
-        lines = pl.ds(pl.multiple_of(block * cells_x, cells_x), cells_x)
+    level = iota((layers, LANES), 0)
+    lane_of = iota((layers, LANES), 1)
+
+    @pl.loop(0, blocks // 2)
+    def _(pair):
+        for n in range(2):
+            block = 2 * pair + n
+            piece = pl.multiple_of(lax.rem(block, pieces) * per_block, per_block)
+            part = profiles[:, :, :, :, pl.ds(piece, per_block), :].reshape(count, LANES)
+            base = lax.div(block, pieces) * layers
+            turned[n] = lax.dot_general(
+                onehot(lane_of == level + base),
+                part,
+                (((1,), (1,)), ((), ())),
+                preferred_element_type=F32,
+            )
+        lines = pl.ds(pl.multiple_of(pair * (2 * count), 2 * count), 2 * count)
         for t in range(tracers):
-            weights = smooth_y[block, t]
-            for k in range(levels):
-                r = t * levels + k
-                left[t, k * cells_y : (k + 1) * cells_y, :] = (
-                    weights * values[r : r + 1, :]
-                ).astype(BF16)
-            acc[t] += dot(left[t], kernel_x_ref[t, lines, :])
+            for n in range(2):
+                weights = smooth_y[2 * pair + n, t]
+                for k in range(levels):
+                    r = t * levels + k
+                    left[t, k * cells_y : (k + 1) * cells_y, n * count : (n + 1) * count] = (
+                        weights * turned[n, r : r + 1, :]
+                    ).astype(BF16)
+            acc[t] += dot(left[t], picked_x[t, lines, :])
 
     mask = mask_ref[...].astype(F32)
     carried = [None] * tracers
@@ -379,9 +404,9 @@
             if k + 1 < levels:
                 carried[t] = acc[t, lines, :] + ratio[k] * carried[t]
             inc_ref[t * levels + k] = (carried[t] * mask).astype(BF16)
+
     store = pltpu.make_async_copy(inc_ref, inc_hbm, store_sem.at[0])
     store.start()
-
     field = inc_ref[...].reshape(layers * cells_y, cells_x)
     found = dot(field, at_own).reshape(layers, cells_y, slots)
     in_row = iota((1, cells_y, slots), 1) == cell_j[None]
@@ -473,9 +498,11 @@
         + [
             pltpu.VMEM((devices, 1, slots), jnp.int32),
             pltpu.VMEM(dims + (slots // 2, LANES), BF16),
+            pltpu.VMEM((blocks, count, LANES), jnp.int32),
+            pltpu.VMEM((tracers, blocks * count, cells_x), BF16),
             pltpu.VMEM((blocks, tracers, cells_y, count), F32),
-            pltpu.VMEM((tracers, levels * cells_y, count), BF16),
-            pltpu.VMEM((LANES, count), F32),
+            pltpu.VMEM((tracers, levels * cells_y, 2 * count), BF16),
+            pltpu.VMEM((2, layers, count), F32),
             pltpu.VMEM((tracers, levels * cells_y, cells_x), F32),
             pltpu.VMEM((levels, cells_y, cells_x), F32),
             pltpu.VMEM((levels, cells_y, cells_x), F32),
@@ -498,7 +525,32 @@
         ),
         name="smooth_profiles",
     )(*operands)
+    parts = 4
+    increment, equivalents = pl.pallas_call(
+        functools.partial(hand_over_kernel, parts),
+        out_shape=(
+            jax.ShapeDtypeStruct(increment.shape, BF16),
+            jax.ShapeDtypeStruct(equivalents.shape, BF16),
+        ),
+        in_specs=[anywhere] * 2,
+        out_specs=(anywhere, anywhere),
+        scratch_shapes=[pltpu.SemaphoreType.DMA((parts + 1,))],
+        compiler_params=pltpu.CompilerParams(vmem_limit_bytes=VMEM_BYTES),
+        name="hand_over",
+    )(increment, equivalents)
     return increment, equivalents[None]
+
+
+def hand_over_kernel(parts, inc_ref, equiv_ref, inc_out, equiv_out, sem):
+    height = inc_ref.shape[0] // parts
+    copies = [pltpu.make_async_copy(equiv_ref, equiv_out, sem.at[parts])]
+    for k in range(parts):
+        lines = pl.ds(k * height, height)
+        copies.append(pltpu.make_async_copy(inc_ref.at[lines], inc_out.at[lines], sem.at[k]))
+    for copy in copies:
+        copy.start()
+    for copy in copies:
+        copy.wait()
 
 
 def plan(devices_x, devices_y, innovations, land_mask, inverse_x, inverse_y):
@@ -515,7 +567,7 @@
         and devices_x % 4 == 0
         and cells_x % LANES == 0
         and cells_x & (cells_x - 1) == 0
-        and cells_x == devices * TILE
+        and cells_x <= 32 * 256
         and inverse_y.shape[1] <= LANES
     )
     return (devices_x // 2, 2, devices_y // 2, 2) if fits else None

time: 40.8 us -> 69.1 us (1.69)
  Pallas kernels: 36.3 us -> 68.3 us
  local copies, waits for them, and re-layouts: 3.59 us -> 0 us
    pallas_call x0 -> x1, Pallas kernels: none -> 33.4 us  [body_gather(): pl.pallas_call(functools.partial(hand_over_kernel, parts), out_shape=(jax...]
    unnamed x2 -> x0, local copies, waits for them, and re-layouts: 3.59 us -> none
    pallas_call x1, Pallas kernels: 36.3 us -> 34.9 us  [body_gather(): pl.pallas_call(functools.partial(profile_kernel, dims, capacity), out_sha...]
where the time goes in v3:
time: 69.1 us; the launch traced here: 68.9 us
  Pallas kernels  68.3 us (99%)
    pallas_call x1, Pallas kernels, body_gather(): pl.pallas_call(functools.partial(profile_kernel, dims, capacity), out_sha...  34.9 us
    pallas_call x1, Pallas kernels, body_gather(): pl.pallas_call(functools.partial(hand_over_kernel, parts), out_shape=(jax...  33.4 us

profile of v3, /device:TPU:0, one launch (start us, length us, event | category | flops | bytes accessed | tf_op | source)
XLA Modules:
  0.0 68.9 jit_solution(5376733335743810676)
XLA Ops:
  0.6 34.9 %smooth_profiles.1 = (bf16[64,16,512]{2,1,0:T(8,128)(2,1)}, bf16[64,128]{1,0:T(8,128)(2,1)}) custom-call(bf16[64,128]{1,0:T(8,128)(2,1)} %bitcast.2, s32[1,128]{1,0:T(1,128)} %columns_hbm.1, s32[1,32]{1,0:T(1,128)} %counts_hbm.1, s32[16,512]{1,0:T(8,128)} %mask_hbm.1, f32[32,16,512]{2,1,0:T(8,128)} %coef_hbm.1, bf16[2,4096,512]{2,1,0:T(8,128)(2,1)} %kernel_x_hbm.1, ...), custom_call_target="tpu_custom_call" | custom-call | tf_op jit(solution)/shard_map/smooth_profiles/pallas_call | solution.py:489
  35.5 33.4 %hand_over.1 = (bf16[64,16,512]{2,1,0:T(8,128)(2,1)}, bf16[64,128]{1,0:T(8,128)(2,1)}) custom-call(bf16[64,16,512]{2,1,0:T(8,128)(2,1)} %get-tuple-element.6.inc_ref, bf16[64,128]{1,0:T(8,128)(2,1)} %get-tuple-element.7.equiv_ref), custom_call_target="tpu_custom_call" | custom-call | tf_op jit(solution)/shard_map/hand_over/pallas_call | solution.py:529

commit v4 on v3

--- a/solution.py
+++ b/solution.py
@@ -206,9 +206,9 @@
 
     barrier = pltpu.get_barrier_semaphore()
 
-    @pl.loop(1, devices)
-    def _(k):
-        pl.semaphore_signal(barrier, inc=1, device_id=place(k)[1], device_id_type=MESH)
+    places = [place(k) for k in range(1, devices)]
+    for _, where in places:
+        pl.semaphore_signal(barrier, inc=1, device_id=where, device_id_type=MESH)
 
     loads[0].wait()
     loads[1].wait()
@@ -220,19 +220,19 @@
     cells[me] = jnp.where(sea > 0.0, columns, -1)
     pl.semaphore_wait(barrier, devices - 1)
 
-    def cell_copy(k):
-        return pltpu.make_async_remote_copy(
+    for _, where in places:
+        pltpu.make_async_remote_copy(
             src_ref=cells.at[me],
             dst_ref=cells.at[me],
-            send_sem=cell_send.at[k - 1],
-            recv_sem=cell_recv.at[k - 1],
-            device_id=place(k)[1],
+            send_sem=cell_send,
+            recv_sem=cell_recv,
+            device_id=where,
             device_id_type=MESH,
-        )
-
-    @pl.loop(1, devices)
-    def _(k):
-        cell_copy(k).start()
+        ).start()
+
+    def all_of(ref, sem):
+        others = ref.at[pl.ds(0, devices - 1)]
+        return pltpu.make_async_copy(others, others, sem)
 
     loads[2].wait()
     loads[3].wait()
@@ -293,9 +293,7 @@
     by_y = send(own_line, along)
     to_twin = [send(own_line, twin)]
 
-    @pl.loop(1, devices)
-    def _(k):
-        cell_copy(k).wait_recv()
+    all_of(cells, cell_recv).wait()
 
     loads[5].wait()
     loads[6].wait()
@@ -416,42 +414,26 @@
         outgoing[d] = picked[d * capacity : (d + 1) * capacity]
     arrived[me] = outgoing[me]
 
-    def back_copy(k):
-        other, where = place(k)
-        return pltpu.make_async_remote_copy(
+    for other, where in places:
+        pltpu.make_async_remote_copy(
             src_ref=outgoing.at[other],
             dst_ref=arrived.at[me],
-            send_sem=back_send.at[k - 1],
-            recv_sem=back_recv.at[k - 1],
+            send_sem=back_send,
+            recv_sem=back_recv,
             device_id=where,
             device_id_type=MESH,
-        )
-
-    @pl.loop(1, devices)
-    def _(k):
-        back_copy(k).start()
-
+        ).start()
     for copy in sent:
         copy.wait_send()
-
-    @pl.loop(1, devices)
-    def _(k):
-        cell_copy(k).wait_send()
-
-    @pl.loop(1, devices)
-    def _(k):
-        back_copy(k).wait_recv()
-
+    all_of(cells, cell_send).wait()
+    all_of(arrived, back_recv).wait()
     for d in range(devices):
         rows[d * capacity : (d + 1) * capacity] = arrived[d]
     equiv_ref[...] = jnp.where(live, rows[...].T[:layers], 0.0).astype(BF16)
     result = pltpu.make_async_copy(equiv_ref, equiv_hbm, store_sem.at[1])
     result.start()
 
-    @pl.loop(1, devices)
-    def _(k):
-        back_copy(k).wait_send()
-
+    all_of(outgoing, back_send).wait()
     store.wait()
     result.wait()
 
@@ -513,12 +495,12 @@
             pltpu.VMEM((layers, slots), BF16),
             pltpu.SemaphoreType.DMA((len(operands),)),
             pltpu.SemaphoreType.DMA((2,)),
-            pltpu.SemaphoreType.DMA((devices - 1,)),
-            pltpu.SemaphoreType.DMA((devices - 1,)),
+            pltpu.SemaphoreType.DMA,
+            pltpu.SemaphoreType.DMA,
             pltpu.SemaphoreType.DMA((n_profile,)),
             pltpu.SemaphoreType.DMA((n_profile,)),
-            pltpu.SemaphoreType.DMA((devices - 1,)),
-            pltpu.SemaphoreType.DMA((devices - 1,)),
+            pltpu.SemaphoreType.DMA,
+            pltpu.SemaphoreType.DMA,
         ],
         compiler_params=pltpu.CompilerParams(
             collective_id=0, has_side_effects=True, vmem_limit_bytes=VMEM_BYTES
@@ -534,22 +516,32 @@
         ),
         in_specs=[anywhere] * 2,
         out_specs=(anywhere, anywhere),
-        scratch_shapes=[pltpu.SemaphoreType.DMA((parts + 1,))],
+        scratch_shapes=[
+            pltpu.VMEM(increment.shape, BF16),
+            pltpu.VMEM(equivalents.shape, BF16),
+            pltpu.SemaphoreType.DMA((2 * (parts + 1),)),
+        ],
         compiler_params=pltpu.CompilerParams(vmem_limit_bytes=VMEM_BYTES),
         name="hand_over",
     )(increment, equivalents)
     return increment, equivalents[None]
 
 
-def hand_over_kernel(parts, inc_ref, equiv_ref, inc_out, equiv_out, sem):
+def hand_over_kernel(parts, inc_ref, equiv_ref, inc_out, equiv_out, inc_held, equiv_held, sem):
     height = inc_ref.shape[0] // parts
-    copies = [pltpu.make_async_copy(equiv_ref, equiv_out, sem.at[parts])]
+    steps = [(equiv_ref, equiv_held, equiv_out)]
     for k in range(parts):
         lines = pl.ds(k * height, height)
-        copies.append(pltpu.make_async_copy(inc_ref.at[lines], inc_out.at[lines], sem.at[k]))
-    for copy in copies:
+        steps.append((inc_ref.at[lines], inc_held.at[lines], inc_out.at[lines]))
+    n = len(steps)
+    ins = [pltpu.make_async_copy(a, b, sem.at[k]) for k, (a, b, _) in enumerate(steps)]
+    outs = [pltpu.make_async_copy(b, c, sem.at[n + k]) for k, (_, b, c) in enumerate(steps)]
+    for copy in ins:
         copy.start()
-    for copy in copies:
+    for first, second in zip(ins, outs):
+        first.wait()
+        second.start()
+    for copy in outs:
         copy.wait()
 
 

time: 69.1 us -> 36.4 us (0.53)
  Pallas kernels: 68.3 us -> 35.5 us
    pallas_call x1, Pallas kernels: 33.4 us -> 2.02 us  [body_gather(): pl.pallas_call(functools.partial(hand_over_kernel, parts), out_shape=(jax...]
    pallas_call x1, Pallas kernels: 34.9 us -> 33.5 us  [body_gather(): pl.pallas_call(functools.partial(profile_kernel, dims, capacity), out_sha...]
where the time goes in v4:
time: 36.4 us; the launch traced here: 36.2 us
  Pallas kernels  35.5 us (98%)
  between operations  0.64 us (2%)
    pallas_call x1, Pallas kernels, body_gather(): pl.pallas_call(functools.partial(profile_kernel, dims, capacity), out_sha...  33.5 us
    pallas_call x1, Pallas kernels, body_gather(): pl.pallas_call(functools.partial(hand_over_kernel, parts), out_shape=(jax...  2.02 us

profile of v4, /device:TPU:0, one launch (start us, length us, event | category | flops | bytes accessed | tf_op | source)
XLA Modules:
  0.0 36.2 jit_solution(8417863509948801144)
XLA Ops:
  0.6 33.5 %smooth_profiles.1 = (bf16[64,16,512]{2,1,0:T(8,128)(2,1)}, bf16[64,128]{1,0:T(8,128)(2,1)}) custom-call(bf16[64,128]{1,0:T(8,128)(2,1)} %bitcast.2, s32[1,128]{1,0:T(1,128)} %columns_hbm.1, s32[1,32]{1,0:T(1,128)} %counts_hbm.1, s32[16,512]{1,0:T(8,128)} %mask_hbm.1, f32[32,16,512]{2,1,0:T(8,128)} %coef_hbm.1, bf16[2,4096,512]{2,1,0:T(8,128)(2,1)} %kernel_x_hbm.1, ...), custom_call_target="tpu_custom_call" | custom-call | tf_op jit(solution)/shard_map/smooth_profiles/pallas_call | solution.py:471
  34.1 2.0 %hand_over.1 = (bf16[64,16,512]{2,1,0:T(8,128)(2,1)}, bf16[64,128]{1,0:T(8,128)(2,1)}) custom-call(bf16[64,16,512]{2,1,0:T(8,128)(2,1)} %get-tuple-element.6.inc_ref, bf16[64,128]{1,0:T(8,128)(2,1)} %get-tuple-element.7.equiv_ref), custom_call_target="tpu_custom_call" | custom-call | tf_op jit(solution)/shard_map/hand_over/pallas_call | solution.py:511

commit v5 on v4

--- a/solution.py
+++ b/solution.py
@@ -182,6 +182,7 @@
     tracers, rows_j, _ = kernel_y_ref.shape
     per_block = devices_y * capacity
     count = devices * per_block
+    by_capacity, by_cells_x = capacity.bit_length() - 1, cells_x.bit_length() - 1
 
     loads = [
         pltpu.make_async_copy(source, target, load_sem.at[k])
@@ -213,7 +214,7 @@
     loads[0].wait()
     loads[1].wait()
     columns = columns_ref[...]
-    cell_i, cell_j = columns & (cells_x - 1), columns // cells_x
+    cell_i, cell_j = columns & (cells_x - 1), columns >> by_cells_x
     at_own = onehot(iota((cells_x, slots), 0) == cell_i)
     masks = dot(mask_ref[...].astype(F32).astype(BF16), at_own)
     sea = jnp.sum(jnp.where(iota((cells_y, slots), 0) == cell_j, masks, 0.0), 0, keepdims=True)
@@ -238,7 +239,7 @@
     loads[3].wait()
     counts = jnp.broadcast_to(counts_ref[...].astype(F32), (8, devices)).astype(BF16)
     lane_count = dot(
-        counts, onehot(iota((devices, slots), 0) == iota((devices, slots), 1) // capacity)
+        counts, onehot(iota((devices, slots), 0) == iota((devices, slots), 1) >> by_capacity)
     )[0:1]
     live = (iota((1, slots), 1) & (capacity - 1)).astype(F32) < lane_count
     values = jnp.where(live, innov_ref[...].astype(F32), 0.0)
@@ -304,11 +305,11 @@
         ).astype(BF16)
         for t in range(tracers)
     ]
-    row = iota((per_block, slots), 0)
-    shape = (devices, per_block, slots)
-    own_lane = iota(shape, 2) == iota(shape, 0) * capacity + (iota(shape, 1) & (capacity - 1))
-    owner = (iota((count, LANES), 0) & (per_block - 1)) // capacity
-    lane = iota((count, LANES), 1)
+    row, lane = iota((per_block, LANES), 0), iota((per_block, LANES), 1)
+    owner = row >> by_capacity
+    first_lane = lane - (row & (capacity - 1))
+    row_lane = lane - owner * cells_y
+    sender = iota((devices, 1, 1), 0) * capacity
     join = jnp.where(iota((2 * slots, LANES), 0) < slots, 32.0, 1.0).astype(BF16)
 
     @pl.loop(0, blocks // 2)
@@ -316,24 +317,27 @@
         for block in (2 * pair, 2 * pair + 1):
             tile = jnp.zeros((per_block, slots), jnp.int32)
             for b in range(devices_y):
-                tile = jnp.where(row // capacity == b, cells[block * devices_y + b], tile)
+                tile = jnp.where(owner == b, cells[block * devices_y + b], tile)
+            own_lane = first_lane[None] == sender
             parts = [
                 jnp.where(own_lane, part.astype(F32)[None], 0.0).reshape(count, slots).astype(BF16)
                 for part in (tile >> 5, tile & 31)
             ]
             cell = dot(jnp.concatenate(parts, axis=1), join).astype(jnp.int32)
             place_x[block] = jnp.where(cell < 0, -1, cell & (cells_x - 1))
-            at_j = onehot(lane == owner * cells_y + cell // cells_x)[:, :rows_j]
+            cell_rows = (cell >> by_cells_x).reshape(devices, per_block, LANES)
+            at_j = onehot(cell_rows == row_lane[None]).reshape(count, LANES)[:, :rows_j]
             for t in range(tracers):
                 smooth_y[block, t] = lax.dot_general(
                     own_y[t], at_j, (((1,), (1,)), ((), ())), preferred_element_type=F32
-                )
+                ).astype(BF16)
 
     def pick_rows(pair):
+        lane_row = iota((1, LANES), 1)
         for block in (2 * pair, 2 * pair + 1):
             column = place_x[block]
             at_i = jnp.concatenate(
-                [onehot(column == lane + start) for start in range(0, cells_x, LANES)], axis=1
+                [onehot(column == lane_row + start) for start in range(0, cells_x, LANES)], axis=1
             )
             lines = pl.ds(pl.multiple_of(block * cells_x, cells_x), cells_x)
             target = pl.ds(pl.multiple_of(block * count, count), count)
@@ -381,9 +385,10 @@
                 weights = smooth_y[2 * pair + n, t]
                 for k in range(levels):
                     r = t * levels + k
+                    value = jnp.broadcast_to(turned[n, r : r + 1, :], weights.shape).astype(BF16)
                     left[t, k * cells_y : (k + 1) * cells_y, n * count : (n + 1) * count] = (
-                        weights * turned[n, r : r + 1, :]
-                    ).astype(BF16)
+                        weights * value
+                    )
             acc[t] += dot(left[t], picked_x[t, lines, :])
 
     mask = mask_ref[...].astype(F32)
@@ -482,7 +487,7 @@
             pltpu.VMEM(dims + (slots // 2, LANES), BF16),
             pltpu.VMEM((blocks, count, LANES), jnp.int32),
             pltpu.VMEM((tracers, blocks * count, cells_x), BF16),
-            pltpu.VMEM((blocks, tracers, cells_y, count), F32),
+            pltpu.VMEM((blocks, tracers, cells_y, count), BF16),
             pltpu.VMEM((tracers, levels * cells_y, 2 * count), BF16),
             pltpu.VMEM((2, layers, count), F32),
             pltpu.VMEM((tracers, levels * cells_y, cells_x), F32),
@@ -554,6 +559,7 @@
         slots == LANES
         and 2 * layers == LANES
         and capacity * devices_y == TILE
+        and slots == devices * capacity
         and devices_x % 2 == 0
         and devices_y == 4
         and devices_x % 4 == 0

time: 36.4 us -> 35.4 us (0.973)
  Pallas kernels: 35.5 us -> 34.5 us
    pallas_call x1, Pallas kernels: 33.5 us -> 32.5 us  [body_gather(): pl.pallas_call(functools.partial(profile_kernel, dims, capacity), out_sha...]
where the time goes in v5:
time: 35.4 us; the launch traced here: 35.2 us
  Pallas kernels  34.5 us (97%)
  between operations  0.64 us (2%)
    pallas_call x1, Pallas kernels, body_gather(): pl.pallas_call(functools.partial(profile_kernel, dims, capacity), out_sha...  32.5 us
    pallas_call x1, Pallas kernels, body_gather(): pl.pallas_call(functools.partial(hand_over_kernel, parts), out_shape=(jax...  2.02 us

profile of v5, /device:TPU:0, one launch (start us, length us, event | category | flops | bytes accessed | tf_op | source)
XLA Modules:
  0.0 35.2 jit_solution(15887943806588285583)
XLA Ops:
  0.6 32.5 %smooth_profiles.1 = (bf16[64,16,512]{2,1,0:T(8,128)(2,1)}, bf16[64,128]{1,0:T(8,128)(2,1)}) custom-call(bf16[64,128]{1,0:T(8,128)(2,1)} %bitcast.2, s32[1,128]{1,0:T(1,128)} %columns_hbm.1, s32[1,32]{1,0:T(1,128)} %counts_hbm.1, s32[16,512]{1,0:T(8,128)} %mask_hbm.1, f32[32,16,512]{2,1,0:T(8,128)} %coef_hbm.1, bf16[2,4096,512]{2,1,0:T(8,128)(2,1)} %kernel_x_hbm.1, ...), custom_call_target="tpu_custom_call" | custom-call | tf_op jit(solution)/shard_map/smooth_profiles/pallas_call | solution.py:476
  33.2 2.0 %hand_over.1 = (bf16[64,16,512]{2,1,0:T(8,128)(2,1)}, bf16[64,128]{1,0:T(8,128)(2,1)}) custom-call(bf16[64,16,512]{2,1,0:T(8,128)(2,1)} %get-tuple-element.6.inc_ref, bf16[64,128]{1,0:T(8,128)(2,1)} %get-tuple-element.7.equiv_ref), custom_call_target="tpu_custom_call" | custom-call | tf_op jit(solution)/shard_map/hand_over/pallas_call | solution.py:516

commit v6 on v5

--- a/solution.py
+++ b/solution.py
@@ -366,10 +366,10 @@
     level = iota((layers, LANES), 0)
     lane_of = iota((layers, LANES), 1)
 
-    @pl.loop(0, blocks // 2)
-    def _(pair):
-        for n in range(2):
-            block = 2 * pair + n
+    @pl.loop(0, blocks // 4)
+    def _(group):
+        for n in range(4):
+            block = 4 * group + n
             piece = pl.multiple_of(lax.rem(block, pieces) * per_block, per_block)
             part = profiles[:, :, :, :, pl.ds(piece, per_block), :].reshape(count, LANES)
             base = lax.div(block, pieces) * layers
@@ -379,10 +379,10 @@
                 (((1,), (1,)), ((), ())),
                 preferred_element_type=F32,
             )
-        lines = pl.ds(pl.multiple_of(pair * (2 * count), 2 * count), 2 * count)
+        lines = pl.ds(pl.multiple_of(group * (4 * count), 4 * count), 4 * count)
         for t in range(tracers):
-            for n in range(2):
-                weights = smooth_y[2 * pair + n, t]
+            for n in range(4):
+                weights = smooth_y[4 * group + n, t]
                 for k in range(levels):
                     r = t * levels + k
                     value = jnp.broadcast_to(turned[n, r : r + 1, :], weights.shape).astype(BF16)
@@ -488,8 +488,8 @@
             pltpu.VMEM((blocks, count, LANES), jnp.int32),
             pltpu.VMEM((tracers, blocks * count, cells_x), BF16),
             pltpu.VMEM((blocks, tracers, cells_y, count), BF16),
-            pltpu.VMEM((tracers, levels * cells_y, 2 * count), BF16),
-            pltpu.VMEM((2, layers, count), F32),
+            pltpu.VMEM((tracers, levels * cells_y, 4 * count), BF16),
+            pltpu.VMEM((4, layers, count), F32),
             pltpu.VMEM((tracers, levels * cells_y, cells_x), F32),
             pltpu.VMEM((levels, cells_y, cells_x), F32),
             pltpu.VMEM((levels, cells_y, cells_x), F32),

time: 35.4 us -> 34.9 us (0.986)
  Pallas kernels: 34.5 us -> 34.1 us
    pallas_call x1, Pallas kernels: 32.5 us -> 32 us  [body_gather(): pl.pallas_call(functools.partial(profile_kernel, dims, capacity), out_sha...]
where the time goes in v6:
time: 34.9 us; the launch traced here: 34.7 us
  Pallas kernels  34.1 us (98%)
  between operations  0.64 us (2%)
    pallas_call x1, Pallas kernels, body_gather(): pl.pallas_call(functools.partial(profile_kernel, dims, capacity), out_sha...  32 us
    pallas_call x1, Pallas kernels, body_gather(): pl.pallas_call(functools.partial(hand_over_kernel, parts), out_shape=(jax...  2.02 us

profile of v6, /device:TPU:0, one launch (start us, length us, event | category | flops | bytes accessed | tf_op | source)
XLA Modules:
  0.0 34.7 jit_solution(16616105963583644153)
XLA Ops:
  0.6 32.0 %smooth_profiles.1 = (bf16[64,16,512]{2,1,0:T(8,128)(2,1)}, bf16[64,128]{1,0:T(8,128)(2,1)}) custom-call(bf16[64,128]{1,0:T(8,128)(2,1)} %bitcast.2, s32[1,128]{1,0:T(1,128)} %columns_hbm.1, s32[1,32]{1,0:T(1,128)} %counts_hbm.1, s32[16,512]{1,0:T(8,128)} %mask_hbm.1, f32[32,16,512]{2,1,0:T(8,128)} %coef_hbm.1, bf16[2,4096,512]{2,1,0:T(8,128)(2,1)} %kernel_x_hbm.1, ...), custom_call_target="tpu_custom_call" | custom-call | tf_op jit(solution)/shard_map/smooth_profiles/pallas_call | solution.py:476
  32.7 2.0 %hand_over.1 = (bf16[64,16,512]{2,1,0:T(8,128)(2,1)}, bf16[64,128]{1,0:T(8,128)(2,1)}) custom-call(bf16[64,16,512]{2,1,0:T(8,128)(2,1)} %get-tuple-element.6.inc_ref, bf16[64,128]{1,0:T(8,128)(2,1)} %get-tuple-element.7.equiv_ref), custom_call_target="tpu_custom_call" | custom-call | tf_op jit(solution)/shard_map/hand_over/pallas_call | solution.py:516
